TPU v7x, 32 devices: a whole 2x2x4 slice. The times are simulated.
32 devices in a mesh: seq: 8 (over z, core), tp: 4 (over y, x).
Axes of the slice: x: 2, y: 2, z: 4, core: 2. Of those that a mesh axis runs over, the one named last changes fastest.
Arguments:
- queries: bfloat16 [512, 8192], P(None, 'tp'), may hold values from -80 to 80
- cache: bfloat16 [2, 8, 8192, 1024], P(None, None, 'seq', 'tp'), may hold values from -6 to 6
- draft_kv: bfloat16 [2, 512, 1024], P(None, 'seq', 'tp'), may hold values from -9 to 9
- out_weight: bfloat16 [8192, 8192], P('tp', 'seq'), may hold values from -0.0625 to 0.0625
- lengths: int32 [8], replicated, may hold values from 508 to 8184, as said below
- parents: int32 [8, 64], replicated, may hold values from -1 to 62, as said below
- path: int32 [8, 8], replicated, may hold values from 0 to 63, as said below
- accepted: int32 [8], replicated, may hold values from 1 to 8
Outputs:
- attn_out: bfloat16 [512, 8192], P('tp', 'seq')
- new_cache: bfloat16 [2, 8, 8192, 1024], P(None, None, 'seq', 'tp')
Inputs may be any that keep to these rules, and one draw needn't show every extreme that they name: `lengths`: request r belongs to tenant t = r mod 4; a request of tenant t holds at most 8192 // 8 * 2 ** t - 8 tokens and at least half of that, and the first request of each tenant holds exactly that many. `parents`: node 0 is the root, with parent -1; every other node i has its parent among the nodes i - 7 to i - 1. `path`: for each request, the nodes of one branch of its tree, each the parent of the next, the last being node 63.
All inputs are finite; a program needn't handle non-finite values.
Results may differ from a plain program's by a relative error of at most 0.0051.
Values may be sent and summed in bfloat16 or wider, within the bound.
No kernel may reach another device: no remote copies, remote signals or barrier semaphores. Data moves between devices by JAX's collectives and lax.ppermute only.
A program may use at most 192 MiB of HBM per device.

v0:
```python
import jax
import jax.numpy as jnp
from jax import lax
from jax.sharding import PartitionSpec as P

HEAD = 128
Q = 64
ACC = 8


masked_score = -1e30


def merged_2(array, axis, combine):
    everything = jax.tree.map(lambda part: lax.all_gather(part, axis), array)
    leading = jax.tree.map(lambda part: part[0], everything)

    def hop(k, so_far):
        return combine(so_far, jax.tree.map(lambda part: part[k], everything))

    return lax.fori_loop(1, lax.axis_size(axis), hop, leading)


def ancestors(parents):
    node_count = parents.shape[1]
    node_ids = jnp.arange(node_count, dtype=jnp.int32)
    step_map = (parents[:, :, None] == node_ids[None, None, :]).astype(jnp.float32)
    identity = jnp.broadcast_to(jnp.eye(node_count, dtype=jnp.float32), step_map.shape)
    reached = jnp.minimum(identity + step_map, 1.0)
    for doubling in range((node_count - 1).bit_length()):
        as_bits = reached.astype(jnp.bfloat16)
        squared = jnp.einsum("nij,njk->nik", as_bits, as_bits, preferred_element_type=jnp.float32)
        reached = jnp.minimum(squared, 1.0)
    return reached


def partial_block(query_rows, key_rows, value_rows, alive_mask):
    scores = jnp.einsum(
        "nqkge,npke->nqkgp", query_rows, key_rows, preferred_element_type=jnp.float32
    ) * HEAD ** (-0.5)
    masked = jnp.where(alive_mask, scores, masked_score)
    peak_score = jnp.max(masked, axis=-1)
    weights = jnp.where(alive_mask, jnp.exp(scores - peak_score[..., None]), 0.0)
    denominator = jnp.sum(weights, axis=-1)
    weighted = jnp.einsum(
        "nqkgp,npke->nqkge",
        weights.astype(jnp.bfloat16),
        value_rows,
        preferred_element_type=jnp.float32,
    )
    return (peak_score, denominator, weighted)


def join_flat(former, latter):
    peak_score = jnp.maximum(former[0], latter[0])
    weight_former = jnp.exp(former[0] - peak_score)
    weight_latter = jnp.exp(latter[0] - peak_score)
    row_count, head_count = peak_score.shape
    weighted = (
        former[2].reshape(row_count, head_count, -1) * weight_former[..., None]
        + latter[2].reshape(row_count, head_count, -1) * weight_latter[..., None]
    )
    return (
        peak_score,
        former[1] * weight_former + latter[1] * weight_latter,
        weighted.reshape(row_count, -1),
    )


def finish(query_flat, draft_rows, family, partials, kv_local):
    node_sets = family.shape[0]
    heads_local = query_flat.shape[1] // HEAD
    group_size = heads_local // kv_local
    reach = ancestors(family)
    query_rows = query_flat.reshape(node_sets, Q, kv_local, group_size, HEAD)
    key_rows = draft_rows[0].reshape(node_sets, Q, kv_local, HEAD)
    value_rows = draft_rows[1].reshape(node_sets, Q, kv_local, HEAD)
    draft_part = partial_block(query_rows, key_rows, value_rows, reach[:, :, None, None, :] > 0.5)
    row_count = node_sets * Q
    draft_part = (
        draft_part[0].reshape(row_count, heads_local),
        draft_part[1].reshape(row_count, heads_local),
        draft_part[2].reshape(row_count, heads_local * HEAD),
    )
    peak_score, denominator, weighted = join_flat(partials, draft_part)
    result = weighted.reshape(row_count, heads_local, HEAD) / denominator[..., None]
    return result.reshape(row_count, heads_local * HEAD).astype(jnp.bfloat16)


def select_rows(draft_rows, branch_path):
    node_sets = branch_path.shape[0]
    draft_table = draft_rows.reshape(2, node_sets, Q, draft_rows.shape[2])
    selector = (branch_path[:, :, None] == jnp.arange(Q, dtype=jnp.int32)[None, None, :]).astype(
        jnp.bfloat16
    )
    return jnp.einsum(
        "naq,xnqd->xnad", selector, draft_table, preferred_element_type=jnp.float32
    ).astype(jnp.bfloat16)


def local(queries, cache, draft_kv, out_weight, lengths, parents, path, accepted):
    seq_index = lax.axis_index("seq")
    requests = cache.shape[1]
    span_cache = cache.shape[2]
    kv_local = cache.shape[3] // HEAD
    heads_local = queries.shape[1] // HEAD
    group_size = heads_local // kv_local
    token_rows = requests * Q
    bundles = requests // 4
    positions = seq_index * span_cache + jnp.arange(span_cache, dtype=jnp.int32)
    alive_mask = positions[None, :] < lengths[:, None]
    query_blocks = queries.reshape(bundles, 4, Q, kv_local, group_size, HEAD)
    key_blocks = cache[0].reshape(bundles, 4, span_cache, kv_local, HEAD)
    value_blocks = cache[1].reshape(bundles, 4, span_cache, kv_local, HEAD)

    def cache_part(inputs):
        query_block, key_block, value_block, alive_block = inputs
        return partial_block(
            query_block, key_block, value_block, alive_block[:, None, None, None, :]
        )

    peak_score, denominator, weighted = lax.map(
        cache_part,
        (query_blocks, key_blocks, value_blocks, alive_mask.reshape(bundles, 4, span_cache)),
    )
    peak_score = peak_score.reshape(token_rows, heads_local)
    denominator = denominator.reshape(token_rows, heads_local)
    weighted = weighted.reshape(token_rows, heads_local * HEAD)
    drafts = lax.all_gather(draft_kv, "seq", axis=1, tiled=True)
    merged = merged_2((peak_score, denominator, weighted), "seq", join_flat)
    attended = finish(queries, drafts, parents, merged, kv_local)
    chosen = select_rows(drafts, path)
    attn_out = lax.psum_scatter(
        jnp.dot(attended, out_weight, preferred_element_type=jnp.float32),
        "tp",
        scatter_dimension=0,
        tiled=True,
    ).astype(jnp.bfloat16)
    offset = positions[None, :] - lengths[:, None]
    writable = (offset >= 0) & (offset < accepted[:, None])
    selector = (
        (offset[:, :, None] == jnp.arange(ACC, dtype=jnp.int32)[None, None, :])
        & writable[:, :, None]
    ).astype(jnp.bfloat16)
    placed = jnp.einsum(
        "rca,xrad->xrcd", selector, chosen, preferred_element_type=jnp.float32
    ).astype(jnp.bfloat16)
    new_cache = jnp.where(writable[None, :, :, None], placed, cache)
    return (attn_out, new_cache)


def solution(mesh):
    return jax.shard_map(
        local,
        mesh=mesh,
        in_specs=(
            P(None, "tp"),
            P(None, None, "seq", "tp"),
            P(None, "seq", "tp"),
            P("tp", "seq"),
            P(),
            P(),
            P(),
            P(),
        ),
        out_specs=(P("tp", "seq"), P(None, None, "seq", "tp")),
        check_vma=False,
    )
```

profile of v0, /device:TPU:0, one launch (start us, length us, event | category | flops | bytes accessed | tf_op | source)
XLA Modules:
  0.0 532.2 jit_solution(2442252458404064533)
XLA Ops:
  8.0 5.8 %fusion.75 = (bf16[1,8,1024,256]{3,2,1,0:T(8,128)(2,1)}, bf16[1,8,1024,256]{3,2,1,0:T(8,128)(2,1)}) fusion(bf16[2,8,1024,256]{3,2,1,0:T(8,128)(2,1)} %param.13), kind=kLoop, calls=%fused_computation.100 | loop fusion | bytes 16777216 | tf_op jit(solution)/shard_map/slice | solution.py:114
  13.8 6.4 %copy.111 = bf16[1,8,1024,256]{2,3,1,0:T(8,128)(2,1)} copy(bf16[1,8,1024,256]{3,2,1,0:T(8,128)(2,1)} %get-tuple-element.304) | data formatting | bytes 8388608
  20.3 6.7 %copy.112 = bf16[1,8,1024,256]{2,3,1,0:T(8,128)(2,1)} copy(bf16[1,8,1024,256]{3,2,1,0:T(8,128)(2,1)} %get-tuple-element.303) | data formatting | bytes 8388608
  28.9 34.6 %while.33 = (s32[]{:T(128)}, f32[2,4,64,2,8]{2,1,0,4,3:T(4,128)S(1)}, f32[2,4,64,2,8]{2,1,0,4,3:T(4,128)S(1)}, f32[2,4,64,2,8,128]{5,4,3,2,1,0:T(8,128)}, pred[2...) while((s32[]{:T(128)}, ...), condition=%wide.region_3.4_spmd, body=%wide.region_0.3_spmd.sunk | while | flops 2193612800 | bytes 64181864 | solution.py:122
  34.6 4.9 fusion.94
  51.9 4.9 fusion.94
  63.5 4.9 all_gather_reshape.11
  69.3 16.7 %all_gather.15 = bf16[2,512,256]{2,1,0:T(8,128)(2,1)S(1)} all-gather(bf16[2,64,256]{2,1,0:T(8,128)(2,1)S(1)} %copy-done.4), channel_id=1, replica_groups=mesh['seq'=8,'tp'=4] {'seq'}, dimensions={1}, use_global_device_ids=true | all-gather | bytes 589824 | tf_op jit(solution)/shard_map/all_gather | solution.py:129
  100.9 5.0 reshape_reshape.3
  105.9 30.3 %all_gather.13 = f32[8,512,16]{1,2,0:T(8,128)S(1)} all-gather(f32[1,512,16]{1,2,0:T(8,128)S(1)} %all_gather_reshape.10), channel_id=1, replica_groups=mesh['seq'=8,'tp'=4] {'seq'}, dimensions={0}, use_global_device_ids=true | all-gather | bytes 294912 | tf_op jit(solution)/shard_map/all_gather | solution.py:15
  136.2 24.8 %all_gather.12 = f32[8,512,16]{1,2,0:T(8,128)S(1)} all-gather(f32[1,512,16]{1,2,0:T(8,128)S(1)} %all_gather_reshape.9), channel_id=1, replica_groups=mesh['seq'=8,'tp'=4] {'seq'}, dimensions={0}, use_global_device_ids=true | all-gather | bytes 294912 | tf_op jit(solution)/shard_map/all_gather | solution.py:15
  161.0 203.1 %all-gather.2.cloned.1.call-done = f32[8,512,2048]{2,1,0:T(8,128)} async-done(((f32[1,512,2048]{2,1,0:T(8,128)}), f32[8,512,2048]{2,1,0:T(8,128)}) %all-gather.2.cloned.1.call-update) | async-done | bytes 33554448 | tf_op jit(solution)/shard_map/all_gather | solution.py:15
  368.8 106.5 %while.34 = (s32[]{:T(128)}, f32[512,16]{0,1:T(8,128)S(1)}, f32[512,16]{0,1:T(8,128)S(1)}, f32[512,2048]{1,0:T(8,128)}, f32[8,512,16]{1,2,0:T(8,128)S(1)}, /*ind...) while((s32[]{:T(128)}, f32[512,16]{0,1:T(8,128)S(1)}, ...), condition=%wide.region_5.6_spmd, body=%wide.region_4.5_spmd.sunk | while | flops 3194885 | bytes 46596272 | solution.py:21
  373.9 10.2 %fusion.96 = f32[512,2048]{1,0:T(8,128)} fusion(f32[64,8,16,128]{3,2,1,0:T(8,128)S(1)} %bitcast.193, f32[512,2048]{1,0:T(8,128)} %get-tuple-element.459, f32[64,8,16,128]{3,2,1,0:T(8,128)S(1)} %bitcast.194, f32[8,512,2048]{2,1,0:T(8,128)} %get-tuple-element.472, s32[]{:T(128)S(6)} %select_n.60), kind=kLoop, calls=%fused_computation.26.clone.1 | loop fusion | flops 3145728 | bytes 20971524 | tf_op jit(solution)/shard_map/while/body/eval_jaxpr/add | solution.py:60
  389.1 10.2 %fusion.96 = f32[512,2048]{1,0:T(8,128)} fusion(f32[64,8,16,128]{3,2,1,0:T(8,128)S(1)} %bitcast.193, f32[512,2048]{1,0:T(8,128)} %get-tuple-element.459, f32[64,8,16,128]{3,2,1,0:T(8,128)S(1)} %bitcast.194, f32[8,512,2048]{2,1,0:T(8,128)} %get-tuple-element.472, s32[]{:T(128)S(6)} %select_n.60), kind=kLoop, calls=%fused_computation.26.clone.1 | loop fusion | flops 3145728 | bytes 20971524 | tf_op jit(solution)/shard_map/while/body/eval_jaxpr/add | solution.py:60
  404.3 10.2 %fusion.96 = f32[512,2048]{1,0:T(8,128)} fusion(f32[64,8,16,128]{3,2,1,0:T(8,128)S(1)} %bitcast.193, f32[512,2048]{1,0:T(8,128)} %get-tuple-element.459, f32[64,8,16,128]{3,2,1,0:T(8,128)S(1)} %bitcast.194, f32[8,512,2048]{2,1,0:T(8,128)} %get-tuple-element.472, s32[]{:T(128)S(6)} %select_n.60), kind=kLoop, calls=%fused_computation.26.clone.1 | loop fusion | flops 3145728 | bytes 20971524 | tf_op jit(solution)/shard_map/while/body/eval_jaxpr/add | solution.py:60
  419.5 10.2 %fusion.96 = f32[512,2048]{1,0:T(8,128)} fusion(f32[64,8,16,128]{3,2,1,0:T(8,128)S(1)} %bitcast.193, f32[512,2048]{1,0:T(8,128)} %get-tuple-element.459, f32[64,8,16,128]{3,2,1,0:T(8,128)S(1)} %bitcast.194, f32[8,512,2048]{2,1,0:T(8,128)} %get-tuple-element.472, s32[]{:T(128)S(6)} %select_n.60), kind=kLoop, calls=%fused_computation.26.clone.1 | loop fusion | flops 3145728 | bytes 20971524 | tf_op jit(solution)/shard_map/while/body/eval_jaxpr/add | solution.py:60
  434.7 10.2 %fusion.96 = f32[512,2048]{1,0:T(8,128)} fusion(f32[64,8,16,128]{3,2,1,0:T(8,128)S(1)} %bitcast.193, f32[512,2048]{1,0:T(8,128)} %get-tuple-element.459, f32[64,8,16,128]{3,2,1,0:T(8,128)S(1)} %bitcast.194, f32[8,512,2048]{2,1,0:T(8,128)} %get-tuple-element.472, s32[]{:T(128)S(6)} %select_n.60), kind=kLoop, calls=%fused_computation.26.clone.1 | loop fusion | flops 3145728 | bytes 20971524 | tf_op jit(solution)/shard_map/while/body/eval_jaxpr/add | solution.py:60
  450.0 10.2 %fusion.96 = f32[512,2048]{1,0:T(8,128)} fusion(f32[64,8,16,128]{3,2,1,0:T(8,128)S(1)} %bitcast.193, f32[512,2048]{1,0:T(8,128)} %get-tuple-element.459, f32[64,8,16,128]{3,2,1,0:T(8,128)S(1)} %bitcast.194, f32[8,512,2048]{2,1,0:T(8,128)} %get-tuple-element.472, s32[]{:T(128)S(6)} %select_n.60), kind=kLoop, calls=%fused_computation.26.clone.1 | loop fusion | flops 3145728 | bytes 20971524 | tf_op jit(solution)/shard_map/while/body/eval_jaxpr/add | solution.py:60
  465.2 10.2 %fusion.96 = f32[512,2048]{1,0:T(8,128)} fusion(f32[64,8,16,128]{3,2,1,0:T(8,128)S(1)} %bitcast.193, f32[512,2048]{1,0:T(8,128)} %get-tuple-element.459, f32[64,8,16,128]{3,2,1,0:T(8,128)S(1)} %bitcast.194, f32[8,512,2048]{2,1,0:T(8,128)} %get-tuple-element.472, s32[]{:T(128)S(6)} %select_n.60), kind=kLoop, calls=%fused_computation.26.clone.1 | loop fusion | flops 3145728 | bytes 20971524 | tf_op jit(solution)/shard_map/while/body/eval_jaxpr/add | solution.py:60
  480.4 9.4 %fusion.34 = f32[512,1024]{1,0:T(8,128)} fusion(bf16[2048,1024]{1,0:T(8,128)(2,1)} %param.15, f32[64,8,16,128]{3,2,1,0:T(8,128)S(1)} %bitcast.201, f32[512,2048]{1,0:T(8,128)S(1)} %copy-done.2, f32[64,8,16,128]{3,2,1,0:T(8,128)S(1)} %bitcast.200, f32[512,2048]{1,0:T(8,128)S(1)} %copy-done.1, f32[64,8,16,128]{3,2,1,0:T(8,128)S(1)} %bitcast.199), kind=kOutput, calls=%fused_computation.51 | convolution fusion | flops 2152726528 | bytes 27262976 | tf_op jit(solution)/shard_map/dot_general | solution.py:134
  489.8 11.4 %copy.90 = bf16[2,8,1024,256]{2,3,0,1:T(8,128)(2,1)} copy(bf16[2,8,1024,256]{3,2,1,0:T(8,128)(2,1)} %param.13) | data formatting | bytes 16777216 | tf_op args[1]
  501.4 7.3 %bitcast_select_fusion.1 = bf16[2,8,1024,256]{2,3,0,1:T(8,128)(2,1)} fusion(bf16[2,8,1024,256]{2,3,0,1:T(8,128)(2,1)} %copy.90, pred[8,1024]{1,0:T(8,128)(4,1)S(1)} %compare_and_fusion, bf16[2,8,64,256]{3,2,1,0:T(8,128)(2,1)S(1)} %bitcast.197, s32[8,1024]{1,0:T(8,128)S(1)} %broadcast_subtract_fusion, s32[8,8]{1,0:T(8,128)S(1)} %copy-done.7), kind=kOutput, calls=%fused_computation.34 | convolution fusion | flops 79859712 | bytes 17342720 | tf_op jit(solution)/shard_map/rca,xrad->xrcd/dot_general | solution.py:145
  508.7 12.3 %copy.91 = bf16[2,8,1024,256]{3,2,1,0:T(8,128)(2,1)} copy(bf16[2,8,1024,256]{2,3,0,1:T(8,128)(2,1)} %bitcast_select_fusion.1) | data formatting | bytes 16777216
  (125 shorter events, 92.6 us)
Async XLA Ops:
  7.2 356.9 %all-gather.2.cloned.1.call-start = ((), (), s32[]{:S(2)}) async-start(), calls=%async_computation.1 | async-start | bytes 37748736 | tf_op jit(solution)/shard_map/all_gather | solution.py:15
  7.3 21.6 %copy-start.5 = (s32[1024]{0:T(1024)}, s32[1024]{0:T(1024)S(1)}, u32[]{:S(2)}) copy-start(s32[1024]{0:T(1024)S(1)} %iota_add_fusion) | copy-start | bytes 12292
  20.2 6.7 %copy-start.3 = (bf16[512,2048]{1,0:T(8,128)(2,1)S(1)}, bf16[512,2048]{1,0:T(8,128)(2,1)}, u32[]{:S(2)}) copy-start(bf16[512,2048]{1,0:T(8,128)(2,1)} %param.12) | copy-start | bytes 6291460
  68.5 0.8 copy-start.4
  68.5 17.7 %copy-start.10 = (s32[8,64]{1,0:T(8,128)S(1)}, s32[8,64]{1,0:T(8,128)}, u32[]{:S(2)}) copy-start(s32[8,64]{1,0:T(8,128)} %param.17) | copy-start | bytes 6148
  68.5 455.1 %reduce-scatter.2.cloned.1.call-start = ((), (), s32[]{:S(2)}) async-start(), calls=%async_computation.2 | async-start | bytes 2621440 | tf_op jit(solution)/shard_map/reduce_scatter | solution.py:133
  371.7 2.2 copy-start
  386.9 2.2 copy-start
  402.1 2.2 copy-start
  417.3 2.2 copy-start
  432.6 2.2 copy-start
  447.8 2.2 copy-start
  463.0 2.2 copy-start
  476.9 2.3 copy-start.1
  476.9 3.5 copy-start.2
  489.8 11.5 %copy-start.6 = (s32[1024]{0:T(1024)S(1)}, s32[1024]{0:T(1024)}, u32[]{:S(2)}) copy-start(s32[1024]{0:T(1024)} %copy-done.5) | copy-start | bytes 12292
  489.8 11.5 %copy-start.8 = (s32[8]{0:T(128)S(1)}, s32[8]{0:T(128)}, u32[]{:S(2)}) copy-start(s32[8]{0:T(128)} %param.16) | copy-start | bytes 100
  489.8 11.4 %copy-start.9 = (s32[8]{0:T(128)S(1)}, s32[8]{0:T(128)}, u32[]{:S(2)}) copy-start(s32[8]{0:T(128)} %param.19) | copy-start | bytes 100
  489.8 11.6 %copy-start.7 = (s32[8,8]{1,0:T(8,128)S(1)}, s32[8,8]{1,0:T(8,128)}, u32[]{:S(2)}) copy-start(s32[8,8]{1,0:T(8,128)} %param.18) | copy-start | bytes 772
Sparse Core Ops, SparseCore 0:
  68.6 295.4 all-gather.1
  489.9 33.6 reduce-scatter.1
where the time goes:
time: 534 us; the launch traced here: 532 us
  waiting for transfers between devices  206 us (39%)
  local copies, waits for them, and re-layouts  114 us (21%)
  other arithmetic  83 us (16%)
  blocking collectives  71.9 us (13%)
  matrix products  42.4 us (8%)
  between operations  14.3 us (3%)
    all_gather x1, waiting for transfers between devices, merged_2(): everything = jax.tree.map(lambda part: lax.all_gather(part, axis), array)  203 us
    add x7, other arithmetic, join_flat(): former[2].reshape(row_count, head_count, -1) * weight_former[..., None]  71.1 us
    all_gather x2, blocking collectives, merged_2(): everything = jax.tree.map(lambda part: lax.all_gather(part, axis), array)  55.1 us
    unnamed x25, local copies, waits for them, and re-layouts  40.5 us
    mul x8, local copies, waits for them, and re-layouts, join_flat(): latter[2].reshape(row_count, head_count, -1) * weight_latter[..., None]  19.2 us
    all_gather x1, blocking collectives, local(): drafts = lax.all_gather(draft_kv, 'seq', axis=1, tiled=True)  16.7 us
    dot_general x3, matrix products, partial_block(): jnp.einsum('nqkge,npke->nqkgp', query_rows, key_rows, preferred_element_t...  12.4 us
    dot_general x3, matrix products, partial_block(): jnp.einsum('nqkgp,npke->nqkge', weights.astype(jnp.bfloat16), value_rows,...  12.1 us
  transfers between devices with their start and end apart: 2, of which 2 were waited for; matrix products, arithmetic and copies ran while one was open for 10% of the time, Pallas kernels for 0%

commit v1 on v0

v1 whole, which is shorter than its diff:
```python
import functools
import math

import jax
import jax.numpy as jnp
from jax import lax
from jax.experimental import pallas as pl
from jax.experimental.pallas import tpu as pltpu
from jax.sharding import PartitionSpec as P

HEAD = 128
Q = 64
ACC = 8
TENANTS = 4
GROUP = 8
DEAD = -1e30
FOLD = HEAD**-0.5 * math.log2(math.e)
WINDOW = 32
BF = jnp.bfloat16
F32 = jnp.float32
VMEM = pl.BlockSpec(memory_space=pltpu.VMEM)
SMEM = pl.BlockSpec(memory_space=pltpu.SMEM)
ANY = pl.BlockSpec(memory_space=pl.ANY)
LIMIT = pltpu.CompilerParams(vmem_limit_bytes=48 * 1024 * 1024)


def dot(a, b, contract=((1,), (0,))):
    return lax.dot_general(a, b, (contract, ((), ())), preferred_element_type=F32)


def live_devices(tenant, n_seq):
    return max(1, n_seq * 2**tenant // 8)


def live_chips(tenant, n_seq):
    return max(1, live_devices(tenant, n_seq) // 2)


def pieces(x):
    high = x.astype(BF).astype(F32)
    middle = (x - high).astype(BF).astype(F32)
    return high, middle, (x - high - middle).astype(BF).astype(F32)


def stat_tile(columns):
    rows = columns[0].shape[0]
    lane = lax.broadcasted_iota(jnp.int32, (rows, HEAD), 1)
    tile = jnp.zeros((rows, HEAD), F32)
    for h, column in enumerate(columns):
        for k, piece in enumerate(pieces(column)):
            tile = jnp.where(lane == k * GROUP + h, piece, tile)
    return tile.astype(BF)


def attend_kernel(tenant, owners, sources, n_sources, *refs):
    len_ref, q_ref, kv_ref, parent_ref = refs[:4]
    drafts = refs[4 : 4 + n_sources]
    mine, theirs, m_s, l_s, acc_s, draft_s = refs[4 + n_sources :]
    span = kv_ref.shape[2]
    heads = q_ref.shape[1] // HEAD // 2
    half = heads * HEAD
    at = pl.program_id(0)
    r = tenant + TENANTS * at
    seq = lax.axis_index("seq")
    core = lax.rem(seq, 2)
    alive = len_ref[r] - seq * span
    owner = jnp.int32(owners[0])
    for k in range(1, len(owners)):
        owner = jnp.where(at == k, owners[k], owner)
    step = 2
    rows = step * Q

    def queries_of(g, h):
        return jnp.concatenate(
            [q_ref[:, (g * heads + h + j) * HEAD : (g * heads + h + j + 1) * HEAD] for j in range(step)], axis=0
        )

    def columns_of(g):
        kv = g * heads // GROUP
        return slice(kv * HEAD, (kv + 1) * HEAD)

    @pl.when(alive > 0)
    def _():
        lane = lax.broadcasted_iota(jnp.int32, (rows, span), 1)
        keep = lane < alive
        for g in range(2):
            keys = kv_ref[0, 0, :, columns_of(g)]
            values = kv_ref[1, 0, :, columns_of(g)]
            for h in range(0, heads, step):
                place = slice((g * heads + h) * Q, (g * heads + h + step) * Q)
                s = jnp.where(keep, dot(queries_of(g, h), keys, ((1,), (1,))), DEAD)
                m = jnp.max(s, axis=1, keepdims=True) * FOLD
                w = jnp.exp2(s * FOLD - m)
                l_s[place] = jnp.broadcast_to(jnp.sum(w, axis=1, keepdims=True), (rows, HEAD))
                m_s[place] = jnp.broadcast_to(m, (rows, HEAD))
                acc_s[place] = dot(w.astype(BF), values)

    @pl.when(alive <= 0)
    def _():
        m_s[...] = jnp.full_like(m_s, DEAD)
        l_s[...] = jnp.zeros_like(l_s)
        acc_s[...] = jnp.zeros_like(acc_s)

    @pl.when(seq == owner)
    def _():
        for k, source in enumerate(sources):

            @pl.when(at == k)
            def _():
                draft_s[...] = drafts[source][...]

        row_id = lax.broadcasted_iota(jnp.int32, (Q, Q), 0)
        column_id = lax.broadcasted_iota(jnp.int32, (Q, Q), 1)
        up = parent_ref[pl.ds(r, 1), :]
        reached = jnp.where((up == row_id) | (row_id == column_id), 1.0, 0.0).astype(BF)
        doublings = (Q - 1).bit_length()
        for k in range(doublings):
            contract = ((0,), (1,)) if k == doublings - 1 else ((1,), (0,))
            reached = jnp.minimum(dot(reached, reached, contract), 1.0).astype(BF)
        reach = jnp.concatenate([reached.astype(F32)] * step, axis=0) > 0.5
        for g in range(2):
            keys = draft_s[0, :, columns_of(g)]
            values = draft_s[1, :, columns_of(g)]
            for h in range(0, heads, step):
                place = slice((g * heads + h) * Q, (g * heads + h + step) * Q)
                s = jnp.where(reach, dot(queries_of(g, h), keys, ((1,), (1,))), DEAD)
                m_old = m_s[place]
                m = jnp.maximum(m_old, jnp.max(s, axis=1, keepdims=True) * FOLD)
                w = jnp.exp2(s * FOLD - m[:, :Q])
                shrink = jnp.exp2(m_old - m)
                l_s[place] = l_s[place] * shrink + jnp.sum(w, axis=1, keepdims=True)
                m_s[place] = m
                acc_s[place] = acc_s[place] * shrink + dot(w.astype(BF), values)

    def finish(g, out):
        stats = []
        for h in range(heads):
            place = slice((g * heads + h) * Q, (g * heads + h + 1) * Q)
            total = l_s[place]
            some = total > 0.0
            total = jnp.where(some, total, 1.0)
            out[:, h * HEAD : (h + 1) * HEAD] = (acc_s[place] / total).astype(BF)
            stats.append(jnp.where(some, m_s[place] + jnp.log2(total), DEAD))
        out[:, half:] = stat_tile(stats)

    for g in range(2):

        @pl.when(core == g)
        def _():
            finish(g, mine)
            finish(1 - g, theirs)


def attend(tenant, n_seq, queries, cache, parents, lengths, drafts, owners, sources):
    requests, span = cache.shape[1], cache.shape[2]
    count = requests // TENANTS
    used = sorted(set(sources))
    width, kv_width = queries.shape[1], cache.shape[3]
    wide = width // 2 + HEAD
    out = jax.ShapeDtypeStruct((count * Q, wide), BF)
    flops = 4 * count * Q * span * width
    return pl.pallas_call(
        functools.partial(attend_kernel, tenant, owners, [used.index(s) for s in sources], len(used)),
        grid_spec=pltpu.PrefetchScalarGridSpec(
            num_scalar_prefetch=1,
            grid=(count,),
            in_specs=[
                pl.BlockSpec((Q, width), lambda i, n: (tenant + TENANTS * i, 0)),
                pl.BlockSpec((2, 1, span, kv_width), lambda i, n: (0, tenant + TENANTS * i, 0, 0)),
                pl.BlockSpec((requests, Q), lambda i, n: (0, 0)),
            ]
            + [pl.BlockSpec((2, Q, kv_width), lambda i, n: (0, 0, 0)) for _ in used],
            out_specs=[pl.BlockSpec((Q, wide), lambda i, n: (i, 0))] * 2,
            scratch_shapes=[
                pltpu.VMEM((Q * width // HEAD, HEAD), F32),
                pltpu.VMEM((Q * width // HEAD, HEAD), F32),
                pltpu.VMEM((Q * width // HEAD, HEAD), F32),
                pltpu.VMEM((2, Q, kv_width), BF),
            ],
        ),
        out_shape=[out, out],
        compiler_params=LIMIT,
        cost_estimate=pl.CostEstimate(
            flops=flops, bytes_accessed=count * (4 * span * kv_width + 4 * Q * width), transcendentals=0
        ),
        name=f"attend_{tenant}",
    )(lengths, queries, cache, parents, *[drafts[s] for s in used])


def combine_kernel(final, a_ref, b_ref, out_ref):
    rows = a_ref.shape[0]
    half = a_ref.shape[1] - HEAD
    heads = half // HEAD

    def stats_of(ref):
        tile = ref[:, half:].astype(F32)
        return tile[:, :GROUP] + tile[:, GROUP : 2 * GROUP] + tile[:, 2 * GROUP : 3 * GROUP]

    a, b = stats_of(a_ref), stats_of(b_ref)
    top = jnp.maximum(a, b)
    weight_a, weight_b = jnp.exp2(a - top), jnp.exp2(b - top)
    total = weight_a + weight_b
    weight_a, weight_b = weight_a / total, weight_b / total
    level = top + jnp.log2(total)
    for h in range(heads):
        place = slice(h * HEAD, (h + 1) * HEAD)
        out_ref[:, place] = (
            a_ref[:, place].astype(F32) * weight_a[:, h : h + 1]
            + b_ref[:, place].astype(F32) * weight_b[:, h : h + 1]
        ).astype(BF)
    if not final:
        out_ref[:, half:] = stat_tile(
            [jnp.broadcast_to(level[:, h : h + 1], (rows, HEAD)) for h in range(heads)]
        )


def combine(a, b, final):
    rows, wide = a.shape
    return pl.pallas_call(
        functools.partial(combine_kernel, final),
        out_shape=jax.ShapeDtypeStruct((rows, wide - HEAD if final else wide), BF),
        in_specs=[VMEM, VMEM],
        out_specs=VMEM,
        compiler_params=LIMIT,
        cost_estimate=pl.CostEstimate(flops=rows * wide * 8, bytes_accessed=rows * wide * 6, transcendentals=0),
        name="combine",
    )(a, b)


def project_kernel(requests, n_tp, tenants, *refs):
    count = len(tenants)
    parts = refs[: 2 * count]
    w_ref = refs[2 * count]
    own_ref, outs, product = refs[2 * count + 1], refs[2 * count + 2 : -1], refs[-1]
    tp = lax.axis_index("tp")
    core = lax.rem(lax.axis_index("seq"), 2)
    half = w_ref.shape[0] // 2
    near = w_ref[pl.ds(pl.multiple_of(core * half, half), half), :]
    far = w_ref[pl.ds(pl.multiple_of((1 - core) * half, half), half), :]
    mine = jnp.concatenate([parts[2 * k][...] for k in range(count)], axis=0)
    other = jnp.concatenate([parts[2 * k + 1][...] for k in range(count)], axis=0)
    product[...] = dot(mine, near) + dot(other, far)
    each = requests // TENANTS
    share = requests // n_tp
    taken = {}
    for k, tenant in enumerate(tenants):
        for i in range(each):
            r = tenant + TENANTS * i
            taken.setdefault(r // share, []).append((r % share, k * each + i))
    for owner in range(n_tp):
        for slot in range(n_tp):

            @pl.when((owner ^ tp) == slot)
            def _():
                for place, (_, block) in enumerate(sorted(taken[owner])):
                    value = product[block * Q : (block + 1) * Q, :]
                    target = own_ref if slot == 0 else outs[slot - 1]
                    target[place * Q : (place + 1) * Q, :] = value.astype(target.dtype)


def project(requests, n_tp, tenants, parts, weight):
    depth, columns = weight.shape
    rows = len(tenants) * (requests // TENANTS) * Q
    mine = rows // n_tp
    steps = 4 if columns % (4 * HEAD) == 0 else 1
    wide = columns // steps
    return pl.pallas_call(
        functools.partial(project_kernel, requests, n_tp, tenants),
        grid=(steps,),
        in_specs=[pl.BlockSpec(part.shape, lambda i: (0, 0)) for part in parts]
        + [pl.BlockSpec((depth, wide), lambda i: (0, i))],
        out_specs=[pl.BlockSpec((mine, wide), lambda i: (0, i))] * n_tp,
        out_shape=[jax.ShapeDtypeStruct((mine, columns), F32)]
        + [jax.ShapeDtypeStruct((mine, columns), BF)] * (n_tp - 1),
        scratch_shapes=[pltpu.VMEM((rows, wide), F32)],
        compiler_params=LIMIT,
        cost_estimate=pl.CostEstimate(
            flops=2 * rows * depth * columns, bytes_accessed=2 * depth * columns, transcendentals=0
        ),
        name="project",
    )(*parts, weight)


def choose_kernel(path_ref, draft_ref, out_ref):
    seq = lax.axis_index("seq")
    row = lax.broadcasted_iota(jnp.int32, (ACC, Q), 0)
    column = lax.broadcasted_iota(jnp.int32, (ACC, Q), 1)
    picked = jnp.zeros((ACC, Q), jnp.int32)
    for j in range(ACC):
        picked = jnp.where(row == j, path_ref[seq, j], picked)
    selector = jnp.where(picked == column, 1.0, 0.0).astype(BF)
    for x in range(2):
        out_ref[0, x] = dot(selector, draft_ref[x]).astype(BF)


def choose(path, draft_kv):
    return pl.pallas_call(
        choose_kernel,
        out_shape=jax.ShapeDtypeStruct((1, 2, ACC, draft_kv.shape[2]), BF),
        in_specs=[SMEM, VMEM],
        out_specs=VMEM,
        compiler_params=LIMIT,
        name="choose",
    )(path, draft_kv)


def copy_kernel(cache_ref, out_ref):
    out_ref[...] = cache_ref[...]


def copied(cache):
    _, requests, span, width = cache.shape
    block = pl.BlockSpec((2, 1, span, width), lambda i: (0, i, 0, 0))
    return pl.pallas_call(
        copy_kernel,
        grid=(requests,),
        out_shape=jax.ShapeDtypeStruct(cache.shape, BF),
        in_specs=[block],
        out_specs=block,
        compiler_params=LIMIT,
        cost_estimate=pl.CostEstimate(flops=0, bytes_accessed=4 * math.prod(cache.shape), transcendentals=0),
        name="copy_cache",
    )(cache)


def patch_kernel(len_ref, accept_ref, cache_ref, chosen_ref, out_ref, window, load_sem, store_sem):
    requests, span = cache_ref.shape[1], cache_ref.shape[2]
    seq = lax.axis_index("seq")

    def place_of(r):
        first = len_ref[r] - seq * span
        start = jnp.clip(first // 16 * 16, 0, span - WINDOW)
        return first, pl.multiple_of(start, 16), (first + ACC > 0) & (first < span)

    def load(r):
        _, start, here = place_of(r)
        return here, pltpu.make_async_copy(
            cache_ref.at[:, r, pl.ds(start, WINDOW), :], window.at[r], load_sem.at[r]
        )

    def store(r):
        _, start, here = place_of(r)
        return here, pltpu.make_async_copy(
            window.at[r], out_ref.at[:, r, pl.ds(start, WINDOW), :], store_sem.at[r]
        )

    for r in range(requests):
        here, copy = load(r)
        pl.when(here)(copy.start)
    for r in range(requests):
        here, copy = load(r)
        first, start, _ = place_of(r)

        @pl.when(here)
        def _():
            copy.wait()
            row = lax.broadcasted_iota(jnp.int32, window.shape[2:], 0) + (start - first)
            for x in range(2):
                value = window[r, x].astype(F32)
                rows = chosen_ref[r ^ seq, x].astype(F32)
                for j in range(ACC):
                    value = jnp.where((row == j) & (j < accept_ref[r]), rows[j : j + 1], value)
                window[r, x] = value.astype(BF)
            store(r)[1].start()

    for r in range(requests):
        here, copy = store(r)
        pl.when(here)(copy.wait)


def patched(cache, chosen, lengths, accepted):
    requests = cache.shape[1]
    return pl.pallas_call(
        patch_kernel,
        out_shape=jax.ShapeDtypeStruct(cache.shape, BF),
        in_specs=[SMEM, SMEM, ANY, VMEM],
        out_specs=ANY,
        scratch_shapes=[
            pltpu.VMEM((requests, 2, WINDOW, cache.shape[3]), BF),
            pltpu.SemaphoreType.DMA((requests,)),
            pltpu.SemaphoreType.DMA((requests,)),
        ],
        input_output_aliases={2: 0},
        compiler_params=LIMIT,
        name="patch_cache",
    )(lengths, accepted, cache, chosen)


def chip_pairs(pairs):
    return [(2 * a + c, 2 * b + c) for a, b in pairs for c in range(2)]


def local(n_seq, n_tp, queries, cache, draft_kv, out_weight, lengths, parents, path, accepted):
    requests = cache.shape[1]
    chips = n_seq // 2
    seq = lax.axis_index("seq")
    chip = seq // 2
    swap_pairs = [(s, s ^ 1) for s in range(n_seq)]

    def swap(array):
        return lax.ppermute(array, "seq", swap_pairs)

    def send(array, pairs):
        return lax.ppermute(array, "seq", chip_pairs(pairs))

    owners, sources, rounds = {}, {}, []
    for r in range(requests):
        owners[r] = r % live_devices(r % TENANTS, n_seq)
        sources[r] = 0
        if owners[r] != r:
            for k, taken in enumerate(rounds):
                if all(owners[r] != b for _, b in taken):
                    break
            else:
                k = len(rounds)
                rounds.append([])
            rounds[k].append((r, owners[r]))
            sources[r] = k + 1
    drafts = [draft_kv] + [lax.ppermute(draft_kv, "seq", pairs) for pairs in rounds]

    def partial_of(tenant):
        own = range(tenant, requests, TENANTS)
        return attend(
            tenant, n_seq, queries, cache, parents, lengths, drafts, [owners[r] for r in own], [sources[r] for r in own]
        )

    def spread(value, first, last):
        held = [value]
        inside = (chip >= first) & (chip <= last)
        newest = value
        while first > 0 or last < chips - 1:
            pairs = []
            if first > 0:
                pairs.append((first, first - 1))
                first -= 1
            if last < chips - 1:
                pairs.append((last, last + 1))
                last += 1
            newest = send(newest, pairs)
            held.append(newest)
        if len(held) == 1:
            return value
        rest = functools.reduce(jnp.add, held[1:])
        return jnp.where(inside, value, rest)

    def reduced(tenant):
        mine, theirs = partial_of(tenant)
        count = live_chips(tenant, n_seq)
        value = combine(mine, swap(theirs), count == 1)
        if count == 1:
            return value, 0, 0
        half = count // 2
        for k in range(half - 1):
            value = combine(value, send(value, [(k, k + 1), (count - 1 - k, count - 2 - k)]), False)
        value = combine(value, send(value, [(half - 1, half), (half, half - 1)]), True)
        return value, half - 1, half

    whole = {}
    for tenant in (3, 2, 0, 1):
        value = spread(*reduced(tenant))
        whole[tenant] = (value, swap(value))

    def sums(tenants):
        parts = [part for tenant in tenants for part in whole[tenant]]
        own, *others = project(requests, n_tp, tenants, parts, out_weight)
        for k, other in enumerate(others):
            arrived = lax.ppermute(other, "tp", [(t, t ^ (k + 1)) for t in range(n_tp)])
            own = own + arrived.astype(F32)
        return own.astype(BF)

    columns = out_weight.shape[1]
    even, odd = (sums(tenants).reshape(-1, Q, columns) for tenants in ((0, 2), (1, 3)))
    attn_out = jnp.stack([even, odd], axis=1).reshape(-1, columns)

    chosen = choose(path, draft_kv)
    distance = 1
    while distance < n_seq:
        arrived = lax.ppermute(chosen, "seq", [(s, s ^ distance) for s in range(n_seq)])
        chosen = jnp.concatenate([chosen, arrived], axis=0)
        distance *= 2
    new_cache = patched(copied(cache), chosen, lengths, accepted)
    return attn_out, new_cache


def solution(mesh):
    return jax.shard_map(
        functools.partial(local, mesh.shape["seq"], mesh.shape["tp"]),
        mesh=mesh,
        in_specs=(
            P(None, "tp"),
            P(None, None, "seq", "tp"),
            P(None, "seq", "tp"),
            P("tp", "seq"),
            P(),
            P(),
            P(),
            P(),
        ),
        out_specs=(P("tp", "seq"), P(None, None, "seq", "tp")),
        check_vma=False,
    )
```

time: 534 us -> 135 us (0.25)
  waiting for transfers between devices: 206 us -> 35.4 us
  local copies, waits for them, and re-layouts: 114 us -> 5.98 us
  other arithmetic: 83 us -> 1.06 us
  blocking collectives: 71.9 us -> 0 us
  Pallas kernels: 0 us -> 57.7 us
  matrix products: 42.4 us -> 0 us
  starting transfers between devices: 0.08 us -> 33.5 us
  between operations: 14.3 us -> 1.05 us
    all_gather x1 -> x0, waiting for transfers between devices: 203 us -> none  [merged_2(): everything = jax.tree.map(lambda part: lax.all_gather(part, axis), array)]
    all_gather x3 -> x0, blocking collectives: 71.9 us -> none  [the longest x2 55.1 us: merged_2(): everything = jax.tree.map(lambda part: lax.all_gather(part, axis), array)]
    add x16 -> x0, other arithmetic: 71.3 us -> none  [the longest x7 71.1 us: join_flat(): former[2].reshape(row_count, head_count, -1) * weight_former[..., None]]
    pallas_call x0 -> x16, Pallas kernels: none -> 57.7 us  [the longest x4 36 us: attend(): pl.pallas_call(functools.partial(attend_kernel, tenant, owners, [used.ind...]
    dot_general x11 -> x0, matrix products: 42.4 us -> none  [the longest x3 12.4 us: partial_block(): jnp.einsum('nqkge,npke->nqkgp', query_rows, key_rows, preferred_element_t...]
    ppermute x0 -> x30, waiting for transfers between devices: none -> 35.4 us  [the longest x12 22.7 us: send(): return lax.ppermute(array, 'seq', chip_pairs(pairs))]
    unnamed x25 -> x18, local copies, waits for them, and re-layouts: 40.5 us -> 5.98 us
    ppermute x0 -> x30, starting transfers between devices: none -> 33.5 us  [the longest x12 12 us: send(): return lax.ppermute(array, 'seq', chip_pairs(pairs))]
  transfers between devices with their start and end apart: 2 -> 30, of which waited for: 2 -> 8; matrix products, arithmetic and copies ran while one was open for 10% -> 0% of each run, Pallas kernels for 0% -> 37%
where the time goes in v1:
time: 135 us
  Pallas kernels  57.7 us (43%)
  waiting for transfers between devices  35.4 us (26%)
  starting transfers between devices  33.5 us (25%)
  local copies, waits for them, and re-layouts  5.98 us (4%)
    pallas_call x4, Pallas kernels, attend(): pl.pallas_call(functools.partial(attend_kernel, tenant, owners, [used.ind...  36 us
    ppermute x12, waiting for transfers between devices, send(): return lax.ppermute(array, 'seq', chip_pairs(pairs))  22.7 us
    ppermute x12, starting transfers between devices, send(): return lax.ppermute(array, 'seq', chip_pairs(pairs))  12 us
    ppermute x3, starting transfers between devices, local(): lax.ppermute(chosen, 'seq', [(s, s ^ distance) for s in range(n_seq)])  9.42 us
    pallas_call x1, Pallas kernels, copied(): pl.pallas_call(copy_kernel, grid=(requests,), out_shape=jax.ShapeDtypeStr...  8.98 us
    ppermute x6, starting transfers between devices, sums(): arrived = lax.ppermute(other, 'tp', [(t, t ^ k + 1) for t in range(n_tp)])  7.33 us
    ppermute x1, waiting for transfers between devices, local(): lax.ppermute(draft_kv, 'seq', pairs)  6.47 us
    ppermute x6, waiting for transfers between devices, sums(): arrived = lax.ppermute(other, 'tp', [(t, t ^ k + 1) for t in range(n_tp)])  6.17 us
  transfers between devices with their start and end apart: 30, of which 8 were waited for; matrix products, arithmetic and copies ran while one was open for 0% of the time, Pallas kernels for 37%

profile of v1, /device:TPU:0, one launch (start us, length us, event | category | flops | bytes accessed | tf_op | source)
XLA Modules:
  0.0 134.7 jit_solution(14699963882438728156)
XLA Ops:
  1.9 6.5 %collective-permute-done.refs_5_ = bf16[2,64,256]{2,1,0:T(8,128)(2,1)S(1)} collective-permute-done((bf16[2,64,256]{2,1,0:T(8,128)(2,1)}, bf16[2,64,256]{2,1,0:T(8,128)(2,1)S(1)}, u32[]{:S(2)}, u32[]{:S(2)}) %collective-permute-start) | collective-permute-done | bytes 65568 | tf_op jit(solution)/shard_map/ppermute | solution.py:419
  8.4 1.6 %copy-done = bf16[512,2048]{1,0:T(8,128)(2,1)S(1)} copy-done((bf16[512,2048]{1,0:T(8,128)(2,1)S(1)}, bf16[512,2048]{1,0:T(8,128)(2,1)}, u32[]{:S(2)}) %copy-start) | copy-done | bytes 2097176
  12.2 8.3 %attend_1.1 = (bf16[128,1152]{1,0:T(8,128)(2,1)S(1)}, bf16[128,1152]{1,0:T(8,128)(2,1)S(1)}) custom-call(s32[8]{0:T(128)S(1)} %copy-done.5, bf16[512,2048]{1,0:T(8,128)(2,1)S(1)} %copy-done, bf16[2,8,1024,256]{3,2,1,0:T(8,128)(2,1)} %cache_ref.1, s32[8,64]{1,0:T(8,128)S(1)} %copy-done.4, bf16[2,64,256]{2,1,0:T(8,128)(2,1)S(1)} %copy-done.3, ...), custom_call_target="tpu_custom_call" | custom-call | flops 1073741824 | bytes 3145728 | tf_op jit(solution)/shard_map/attend_1/pallas_call | solution.py:162
  22.0 8.3 %attend_3.1 = (bf16[128,1152]{1,0:T(8,128)(2,1)S(1)}, bf16[128,1152]{1,0:T(8,128)(2,1)S(1)}) custom-call(s32[8]{0:T(128)S(1)} %copy-done.5, bf16[512,2048]{1,0:T(8,128)(2,1)S(1)} %copy-done, bf16[2,8,1024,256]{3,2,1,0:T(8,128)(2,1)} %cache_ref.1, s32[8,64]{1,0:T(8,128)S(1)} %copy-done.4, bf16[2,64,256]{2,1,0:T(8,128)(2,1)S(1)} %copy-done.3), custom_call_target="tpu_custom_call" | custom-call | flops 1073741824 | bytes 3145728 | tf_op jit(solution)/shard_map/attend_3/pallas_call | solution.py:162
  30.5 10.8 %attend_0.1 = (bf16[128,1152]{1,0:T(8,128)(2,1)S(1)}, bf16[128,1152]{1,0:T(8,128)(2,1)S(1)}) custom-call(s32[8]{0:T(128)S(1)} %copy-done.5, bf16[512,2048]{1,0:T(8,128)(2,1)S(1)} %copy-done, bf16[2,8,1024,256]{3,2,1,0:T(8,128)(2,1)} %cache_ref.1, s32[8,64]{1,0:T(8,128)S(1)} %copy-done.4, bf16[2,64,256]{2,1,0:T(8,128)(2,1)S(1)} %copy-done.3, ...), custom_call_target="tpu_custom_call" | custom-call | flops 1073741824 | bytes 3145728 | tf_op jit(solution)/shard_map/attend_0/pallas_call | solution.py:162
  41.4 8.5 %attend_2.1 = (bf16[128,1152]{1,0:T(8,128)(2,1)S(1)}, bf16[128,1152]{1,0:T(8,128)(2,1)S(1)}) custom-call(s32[8]{0:T(128)S(1)} %copy-done.5, bf16[512,2048]{1,0:T(8,128)(2,1)S(1)} %copy-done, bf16[2,8,1024,256]{3,2,1,0:T(8,128)(2,1)} %cache_ref.1, s32[8,64]{1,0:T(8,128)S(1)} %copy-done.4, bf16[2,64,256]{2,1,0:T(8,128)(2,1)S(1)} %copy-done.3, ...), custom_call_target="tpu_custom_call" | custom-call | flops 1073741824 | bytes 3145728 | tf_op jit(solution)/shard_map/attend_2/pallas_call | solution.py:162
  56.8 1.9 %collective-permute-start.7 = (bf16[128,1152]{1,0:T(8,128)(2,1)S(1)}, bf16[128,1152]{1,0:T(8,128)(2,1)S(1)}, u32[]{:S(2)}, u32[]{:S(2)}) collective-permute-start(bf16[128,1152]{1,0:T(8,128)(2,1)S(1)} %combine.8.a_ref), channel_id=1, source_target_pairs={{0,8},{4,12},{8,0},{12,4},{1,9},{5,13},{9,1},{13,5},{2,10},{6,14},... | collective-permute-start | bytes 884744 | tf_op jit(solution)/shard_map/ppermute | solution.py:404
  59.6 4.9 %collective-permute-done.2 = bf16[128,1024]{1,0:T(8,128)(2,1)S(1)} collective-permute-done((bf16[128,1024]{1,0:T(8,128)(2,1)S(1)}, bf16[128,1024]{1,0:T(8,128)(2,1)S(1)}, u32[]{:S(2)}, u32[]{:S(2)}) %collective-permute-start.2) | collective-permute-done | bytes 262176 | tf_op jit(solution)/shard_map/ppermute | solution.py:404
  65.2 5.6 %collective-permute-done.20.b_ref = bf16[128,1152]{1,0:T(8,128)(2,1)S(1)} collective-permute-done((bf16[128,1152]{1,0:T(8,128)(2,1)S(1)}, bf16[128,1152]{1,0:T(8,128)(2,1)S(1)}, u32[]{:S(2)}, u32[]{:S(2)}) %collective-permute-start.20) | collective-permute-done | bytes 294944 | tf_op jit(solution)/shard_map/ppermute | solution.py:404
  72.2 4.4 %collective-permute-done.7.b_ref = bf16[128,1152]{1,0:T(8,128)(2,1)S(1)} collective-permute-done((bf16[128,1152]{1,0:T(8,128)(2,1)S(1)}, bf16[128,1152]{1,0:T(8,128)(2,1)S(1)}, u32[]{:S(2)}, u32[]{:S(2)}) %collective-permute-start.7) | collective-permute-done | bytes 294944 | tf_op jit(solution)/shard_map/ppermute | solution.py:404
  79.1 9.0 %copy_cache.1.cache_ref = bf16[2,8,1024,256]{3,2,1,0:T(8,128)(2,1)} custom-call(bf16[2,8,1024,256]{3,2,1,0:T(8,128)(2,1)} %cache_ref.1), custom_call_target="tpu_custom_call" | custom-call | bytes 16777216 | tf_op jit(solution)/shard_map/copy_cache/pallas_call | solution.py:314
  89.0 3.2 %collective-permute-start.28 = (bf16[2,2,8,256]{3,2,1,0:T(8,128)(2,1)S(1)}, bf16[2,2,8,256]{3,2,1,0:T(8,128)(2,1)S(1)}, u32[]{:S(2)}, u32[]{:S(2)}) collective-permute-start(bf16[2,2,8,256]{3,2,1,0:T(8,128)(2,1)S(1)} %pad_maximum_fusion.3), channel_id=1, source_target_pairs={{0,8},{4,12},{8,0},{12,4},{16,24},{20,28},{24,16},{28,20},{1,9},{5... | collective-permute-start | bytes 49160 | tf_op jit(solution)/shard_map/ppermute | solution.py:478
  95.4 7.6 %collective-permute-done.22 = bf16[128,1024]{1,0:T(8,128)(2,1)S(1)} collective-permute-done((bf16[128,1024]{1,0:T(8,128)(2,1)S(1)}, bf16[128,1024]{1,0:T(8,128)(2,1)S(1)}, u32[]{:S(2)}, u32[]{:S(2)}) %collective-permute-start.22) | collective-permute-done | bytes 262176 | tf_op jit(solution)/shard_map/ppermute | solution.py:404
  103.7 6.2 %collective-permute-start.29 = (bf16[4,2,8,256]{3,2,1,0:T(8,128)(2,1)S(1)}, bf16[4,2,8,256]{3,2,1,0:T(8,128)(2,1)S(1)}, u32[]{:S(2)}, u32[]{:S(2)}) collective-permute-start(bf16[4,2,8,256]{3,2,1,0:T(8,128)(2,1)S(1)} %pad_maximum_fusion.2), channel_id=1, source_target_pairs={{0,16},{4,20},{8,24},{12,28},{16,0},{20,4},{24,8},{28,12},{1,17},{... | collective-permute-start | bytes 98312 | tf_op jit(solution)/shard_map/ppermute | solution.py:478
  109.9 2.2 %copy-done.1 = bf16[2048,1024]{1,0:T(8,128)(2,1)S(1)} copy-done((bf16[2048,1024]{1,0:T(8,128)(2,1)S(1)}, bf16[2048,1024]{1,0:T(8,128)(2,1)}, u32[]{:S(2)}) %copy-start.1) | copy-done | bytes 4194328
  112.1 2.8 %project.3 = (f32[64,1024]{1,0:T(8,128)S(1)}, bf16[64,1024]{1,0:T(8,128)(2,1)S(1)}, bf16[64,1024]{1,0:T(8,128)(2,1)S(1)}, bf16[64,1024]{1,0:T(8,128)(2,1)S(1)}) custom-call(bf16[128,1024]{1,0:T(8,128)(2,1)S(1)} %add_select_fusion.refs_0_, bf16[128,1024]{1,0:T(8,128)(2,1)S(1)} %collective-permute-done.18.refs_1_, ...), custom_call_target="tpu_custom_call" | custom-call | flops 1073741824 | bytes 4194304 | tf_op jit(solution)/shard_map/project/pallas_call | solution.py:267
  114.9 2.2 %collective-permute-start.24 = (bf16[64,1024]{1,0:T(8,128)(2,1)S(1)}, bf16[64,1024]{1,0:T(8,128)(2,1)S(1)}, u32[]{:S(2)}, u32[]{:S(2)}) collective-permute-start(bf16[64,1024]{1,0:T(8,128)(2,1)S(1)} %get-tuple-element.31), channel_id=1, source_target_pairs={{0,1},{1,0},{2,3},{3,2},{4,5},{5,4},{6,7},{7,6},{8,9},{9,8},{10,11... | collective-permute-start | bytes 393224 | tf_op jit(solution)/shard_map/ppermute | solution.py:467
  117.2 1.5 %collective-permute-start.25 = (bf16[64,1024]{1,0:T(8,128)(2,1)S(1)}, bf16[64,1024]{1,0:T(8,128)(2,1)S(1)}, u32[]{:S(2)}, u32[]{:S(2)}) collective-permute-start(bf16[64,1024]{1,0:T(8,128)(2,1)S(1)} %get-tuple-element.32), channel_id=1, source_target_pairs={{0,2},{1,3},{2,0},{3,1},{4,6},{5,7},{6,4},{7,5},{8,10},{9,11},{10,... | collective-permute-start | bytes 393224 | tf_op jit(solution)/shard_map/ppermute | solution.py:467
  118.7 2.5 %patch_cache.1 = bf16[2,8,1024,256]{3,2,1,0:T(8,128)(2,1)} custom-call(s32[8]{0:T(128)S(1)} %copy-done.6, s32[8]{0:T(128)S(1)} %copy-done.8, bf16[2,8,1024,256]{3,2,1,0:T(8,128)(2,1)} %copy_cache.1.cache_ref, bf16[8,2,8,256]{3,2,1,0:T(8,128)(2,1)S(1)} %pad_maximum_fusion.1.chosen_ref), custom_call_target="tpu_custom_call", output_to_operand_aliasing={{}: (2, {})} | custom-call | tf_op jit(solution)/shard_map/patch_cache/pallas_call | solution.py:373
  121.3 2.8 %project.2 = (f32[64,1024]{1,0:T(8,128)S(1)}, bf16[64,1024]{1,0:T(8,128)(2,1)S(1)}, bf16[64,1024]{1,0:T(8,128)(2,1)S(1)}, bf16[64,1024]{1,0:T(8,128)(2,1)S(1)}) custom-call(bf16[128,1024]{1,0:T(8,128)(2,1)S(1)} %add_select_fusion.2.refs_0_, bf16[128,1024]{1,0:T(8,128)(2,1)S(1)} %collective-permute-done.5.refs_1_, ...), custom_call_target="tpu_custom_call" | custom-call | flops 1073741824 | bytes 4194304 | tf_op jit(solution)/shard_map/project/pallas_call | solution.py:267
  124.1 2.0 %collective-permute-start.11 = (bf16[64,1024]{1,0:T(8,128)(2,1)S(1)}, bf16[64,1024]{1,0:T(8,128)(2,1)S(1)}, u32[]{:S(2)}, u32[]{:S(2)}) collective-permute-start(bf16[64,1024]{1,0:T(8,128)(2,1)S(1)} %get-tuple-element.23), channel_id=1, source_target_pairs={{0,1},{1,0},{2,3},{3,2},{4,5},{5,4},{6,7},{7,6},{8,9},{9,8},{10,11... | collective-permute-start | bytes 393224 | tf_op jit(solution)/shard_map/ppermute | solution.py:467
  126.1 1.5 %collective-permute-start.12 = (bf16[64,1024]{1,0:T(8,128)(2,1)S(1)}, bf16[64,1024]{1,0:T(8,128)(2,1)S(1)}, u32[]{:S(2)}, u32[]{:S(2)}) collective-permute-start(bf16[64,1024]{1,0:T(8,128)(2,1)S(1)} %get-tuple-element.24), channel_id=1, source_target_pairs={{0,2},{1,3},{2,0},{3,1},{4,6},{5,7},{6,4},{7,5},{8,10},{9,11},{10,... | collective-permute-start | bytes 393224 | tf_op jit(solution)/shard_map/ppermute | solution.py:467
  127.7 2.1 %collective-permute-done.11 = bf16[64,1024]{1,0:T(8,128)(2,1)S(1)} collective-permute-done((bf16[64,1024]{1,0:T(8,128)(2,1)S(1)}, bf16[64,1024]{1,0:T(8,128)(2,1)S(1)}, u32[]{:S(2)}, u32[]{:S(2)}) %collective-permute-start.11) | collective-permute-done | bytes 131104 | tf_op jit(solution)/shard_map/ppermute | solution.py:467
  129.8 4.1 %collective-permute-done.12 = bf16[64,1024]{1,0:T(8,128)(2,1)S(1)} collective-permute-done((bf16[64,1024]{1,0:T(8,128)(2,1)S(1)}, bf16[64,1024]{1,0:T(8,128)(2,1)S(1)}, u32[]{:S(2)}, u32[]{:S(2)}) %collective-permute-start.12) | collective-permute-done | bytes 131104 | tf_op jit(solution)/shard_map/ppermute | solution.py:467
  (80 shorter events, 23.0 us)
Async XLA Ops:
  20.5 30.0 %collective-permute-start.14 = (bf16[128,1152]{1,0:T(8,128)(2,1)S(1)}, bf16[128,1152]{1,0:T(8,128)(2,1)S(1)}, u32[]{:S(2)}, u32[]{:S(2)}) collective-permute-start(bf16[128,1152]{1,0:T(8,128)(2,1)S(1)} %get-tuple-element.27), channel_id=1, source_target_pairs={{0,4},{4,0},{8,12},{12,8},{16,20},{20,16},{24,28},{28,24},{1,5},{5... | collective-permute-start | bytes 884744 | tf_op jit(solution)/shard_map/ppermute | solution.py:401
  30.4 23.7 %collective-permute-start.19 = (bf16[128,1152]{1,0:T(8,128)(2,1)S(1)}, bf16[128,1152]{1,0:T(8,128)(2,1)S(1)}, u32[]{:S(2)}, u32[]{:S(2)}) collective-permute-start(bf16[128,1152]{1,0:T(8,128)(2,1)S(1)} %get-tuple-element.29), channel_id=1, source_target_pairs={{0,4},{4,0},{8,12},{12,8},{16,20},{20,16},{24,28},{28,24},{1,5},{5... | collective-permute-start | bytes 884744 | tf_op jit(solution)/shard_map/ppermute | solution.py:401
  41.3 11.0 %collective-permute-start.1 = (bf16[128,1152]{1,0:T(8,128)(2,1)S(1)}, bf16[128,1152]{1,0:T(8,128)(2,1)S(1)}, u32[]{:S(2)}, u32[]{:S(2)}) collective-permute-start(bf16[128,1152]{1,0:T(8,128)(2,1)S(1)} %get-tuple-element.19), channel_id=1, source_target_pairs={{0,4},{4,0},{8,12},{12,8},{16,20},{20,16},{24,28},{28,24},{1,5},{5... | collective-permute-start | bytes 884744 | tf_op jit(solution)/shard_map/ppermute | solution.py:401
  51.0 7.9 %collective-permute-start.15 = (bf16[128,1024]{1,0:T(8,128)(2,1)S(1)}, bf16[128,1024]{1,0:T(8,128)(2,1)S(1)}, u32[]{:S(2)}, u32[]{:S(2)}) collective-permute-start(bf16[128,1024]{1,0:T(8,128)(2,1)S(1)} %combine.10), channel_id=1, source_target_pairs={{0,8},{4,12},{1,9},{5,13},{2,10},{6,14},{3,11},{7,15}} | collective-permute-start | bytes 786440 | tf_op jit(solution)/shard_map/ppermute | solution.py:404
  52.8 11.7 %collective-permute-start.2 = (bf16[128,1024]{1,0:T(8,128)(2,1)S(1)}, bf16[128,1024]{1,0:T(8,128)(2,1)S(1)}, u32[]{:S(2)}, u32[]{:S(2)}) collective-permute-start(bf16[128,1024]{1,0:T(8,128)(2,1)S(1)} %combine.7), channel_id=1, source_target_pairs={{0,8},{4,12},{1,9},{5,13},{2,10},{6,14},{3,11},{7,15}} | collective-permute-start | bytes 786440 | tf_op jit(solution)/shard_map/ppermute | solution.py:404
  54.8 16.1 %collective-permute-start.20 = (bf16[128,1152]{1,0:T(8,128)(2,1)S(1)}, bf16[128,1152]{1,0:T(8,128)(2,1)S(1)}, u32[]{:S(2)}, u32[]{:S(2)}) collective-permute-start(bf16[128,1152]{1,0:T(8,128)(2,1)S(1)} %combine.11.a_ref), channel_id=1, source_target_pairs={{0,8},{4,12},{24,16},{28,20},{1,9},{5,13},{25,17},{29,21},{2,10},{... | collective-permute-start | bytes 884744 | tf_op jit(solution)/shard_map/ppermute | solution.py:404
  56.8 19.8 %collective-permute-start.7 = (bf16[128,1152]{1,0:T(8,128)(2,1)S(1)}, bf16[128,1152]{1,0:T(8,128)(2,1)S(1)}, u32[]{:S(2)}, u32[]{:S(2)}) collective-permute-start(bf16[128,1152]{1,0:T(8,128)(2,1)S(1)} %combine.8.a_ref), channel_id=1, source_target_pairs={{0,8},{4,12},{8,0},{12,4},{1,9},{5,13},{9,1},{13,5},{2,10},{6,14},... | collective-permute-start | bytes 884744 | tf_op jit(solution)/shard_map/ppermute | solution.py:404
  58.9 18.8 %collective-permute-start.16 = (bf16[128,1024]{1,0:T(8,128)(2,1)S(1)}, bf16[128,1024]{1,0:T(8,128)(2,1)S(1)}, u32[]{:S(2)}, u32[]{:S(2)}) collective-permute-start(bf16[128,1024]{1,0:T(8,128)(2,1)S(1)} %collective-permute-done.15), channel_id=1, source_target_pairs={{8,16},{12,20},{9,17},{13,21},{10,18},{14,22},{11,19},{15,23}} | collective-permute-start | bytes 786440 | tf_op jit(solution)/shard_map/ppermute | solution.py:404
  64.5 23.6 %collective-permute-start.3 = (bf16[128,1024]{1,0:T(8,128)(2,1)S(1)}, bf16[128,1024]{1,0:T(8,128)(2,1)S(1)}, u32[]{:S(2)}, u32[]{:S(2)}) collective-permute-start(bf16[128,1024]{1,0:T(8,128)(2,1)S(1)} %collective-permute-done.2), channel_id=1, source_target_pairs={{8,16},{12,20},{9,17},{13,21},{10,18},{14,22},{11,19},{15,23}} | collective-permute-start | bytes 786440 | tf_op jit(solution)/shard_map/ppermute | solution.py:404
  71.5 20.7 %collective-permute-start.21 = (bf16[128,1152]{1,0:T(8,128)(2,1)S(1)}, bf16[128,1152]{1,0:T(8,128)(2,1)S(1)}, u32[]{:S(2)}, u32[]{:S(2)}) collective-permute-start(bf16[128,1152]{1,0:T(8,128)(2,1)S(1)} %combine.12.a_ref), channel_id=1, source_target_pairs={{8,16},{12,20},{16,8},{20,12},{9,17},{13,21},{17,9},{21,13},{10,18... | collective-permute-start | bytes 884744 | tf_op jit(solution)/shard_map/ppermute | solution.py:404
  77.0 16.9 %collective-permute-start.8 = (bf16[128,1024]{1,0:T(8,128)(2,1)S(1)}, bf16[128,1024]{1,0:T(8,128)(2,1)S(1)}, u32[]{:S(2)}, u32[]{:S(2)}) collective-permute-start(bf16[128,1024]{1,0:T(8,128)(2,1)S(1)} %combine.9), channel_id=1, source_target_pairs={{8,16},{12,20},{9,17},{13,21},{10,18},{14,22},{11,19},{15,23}} | collective-permute-start | bytes 786440 | tf_op jit(solution)/shard_map/ppermute | solution.py:404
  77.7 16.9 %collective-permute-start.17 = (bf16[128,1024]{1,0:T(8,128)(2,1)S(1)}, bf16[128,1024]{1,0:T(8,128)(2,1)S(1)}, u32[]{:S(2)}, u32[]{:S(2)}) collective-permute-start(bf16[128,1024]{1,0:T(8,128)(2,1)S(1)} %collective-permute-done.16), channel_id=1, source_target_pairs={{16,24},{20,28},{17,25},{21,29},{18,26},{22,30},{19,27},{23,31}} | collective-permute-start | bytes 786440 | tf_op jit(solution)/shard_map/ppermute | solution.py:404
  79.1 9.8 %collective-permute-start.27 = (bf16[1,2,8,256]{3,2,1,0:T(8,128)(2,1)S(1)}, bf16[1,2,8,256]{3,2,1,0:T(8,128)(2,1)S(1)}, u32[]{:S(2)}, u32[]{:S(2)}) collective-permute-start(bf16[1,2,8,256]{3,2,1,0:T(8,128)(2,1)S(1)} %choose.1), channel_id=1, source_target_pairs={{0,4},{4,0},{8,12},{12,8},{16,20},{20,16},{24,28},{28,24},{1,5},{5... | collective-permute-start | bytes 24584 | tf_op jit(solution)/shard_map/ppermute | solution.py:478
  89.0 14.7 %collective-permute-start.28 = (bf16[2,2,8,256]{3,2,1,0:T(8,128)(2,1)S(1)}, bf16[2,2,8,256]{3,2,1,0:T(8,128)(2,1)S(1)}, u32[]{:S(2)}, u32[]{:S(2)}) collective-permute-start(bf16[2,2,8,256]{3,2,1,0:T(8,128)(2,1)S(1)} %pad_maximum_fusion.3), channel_id=1, source_target_pairs={{0,8},{4,12},{8,0},{12,4},{16,24},{20,28},{24,16},{28,20},{1,9},{5... | collective-permute-start | bytes 49160 | tf_op jit(solution)/shard_map/ppermute | solution.py:478
  92.6 10.3 %collective-permute-start.22 = (bf16[128,1024]{1,0:T(8,128)(2,1)S(1)}, bf16[128,1024]{1,0:T(8,128)(2,1)S(1)}, u32[]{:S(2)}, u32[]{:S(2)}) collective-permute-start(bf16[128,1024]{1,0:T(8,128)(2,1)S(1)} %combine.13), channel_id=1, source_target_pairs={{8,0},{12,4},{16,24},{20,28},{9,1},{13,5},{17,25},{21,29},{10,2},{... | collective-permute-start | bytes 786440 | tf_op jit(solution)/shard_map/ppermute | solution.py:404
  93.9 9.1 %collective-permute-start.9 = (bf16[128,1024]{1,0:T(8,128)(2,1)S(1)}, bf16[128,1024]{1,0:T(8,128)(2,1)S(1)}, u32[]{:S(2)}, u32[]{:S(2)}) collective-permute-start(bf16[128,1024]{1,0:T(8,128)(2,1)S(1)} %collective-permute-done.8), channel_id=1, source_target_pairs={{16,24},{20,28},{17,25},{21,29},{18,26},{22,30},{19,27},{23,31}} | collective-permute-start | bytes 786440 | tf_op jit(solution)/shard_map/ppermute | solution.py:404
  94.7 15.2 %collective-permute-start.18 = (bf16[128,1024]{1,0:T(8,128)(2,1)S(1)}, bf16[128,1024]{1,0:T(8,128)(2,1)S(1)}, u32[]{:S(2)}, u32[]{:S(2)}) collective-permute-start(bf16[128,1024]{1,0:T(8,128)(2,1)S(1)} %add_select_fusion.refs_0_), channel_id=1, source_target_pairs={{0,4},{4,0},{8,12},{12,8},{16,20},{20,16},{24,28},{28,24},{1,5},{5... | collective-permute-start | bytes 786440 | tf_op jit(solution)/shard_map/ppermute | solution.py:401
  95.0 26.2 %collective-permute-start.5 = (bf16[128,1024]{1,0:T(8,128)(2,1)S(1)}, bf16[128,1024]{1,0:T(8,128)(2,1)S(1)}, u32[]{:S(2)}, u32[]{:S(2)}) collective-permute-start(bf16[128,1024]{1,0:T(8,128)(2,1)S(1)} %add_select_fusion.2.refs_0_), channel_id=1, source_target_pairs={{0,4},{4,0},{8,12},{12,8},{16,20},{20,16},{24,28},{28,24},{1,5},{5... | collective-permute-start | bytes 786440 | tf_op jit(solution)/shard_map/ppermute | solution.py:401
  103.1 18.1 %collective-permute-start.10 = (bf16[128,1024]{1,0:T(8,128)(2,1)S(1)}, bf16[128,1024]{1,0:T(8,128)(2,1)S(1)}, u32[]{:S(2)}, u32[]{:S(2)}) collective-permute-start(bf16[128,1024]{1,0:T(8,128)(2,1)S(1)} %add_select_fusion.1.refs_2_), channel_id=1, source_target_pairs={{0,4},{4,0},{8,12},{12,8},{16,20},{20,16},{24,28},{28,24},{1,5},{5... | collective-permute-start | bytes 786440 | tf_op jit(solution)/shard_map/ppermute | solution.py:401
  103.7 15.0 %collective-permute-start.29 = (bf16[4,2,8,256]{3,2,1,0:T(8,128)(2,1)S(1)}, bf16[4,2,8,256]{3,2,1,0:T(8,128)(2,1)S(1)}, u32[]{:S(2)}, u32[]{:S(2)}) collective-permute-start(bf16[4,2,8,256]{3,2,1,0:T(8,128)(2,1)S(1)} %pad_maximum_fusion.2), channel_id=1, source_target_pairs={{0,16},{4,20},{8,24},{12,28},{16,0},{20,4},{24,8},{28,12},{1,17},{... | collective-permute-start | bytes 98312 | tf_op jit(solution)/shard_map/ppermute | solution.py:478
  114.9 12.7 %collective-permute-start.24 = (bf16[64,1024]{1,0:T(8,128)(2,1)S(1)}, bf16[64,1024]{1,0:T(8,128)(2,1)S(1)}, u32[]{:S(2)}, u32[]{:S(2)}) collective-permute-start(bf16[64,1024]{1,0:T(8,128)(2,1)S(1)} %get-tuple-element.31), channel_id=1, source_target_pairs={{0,1},{1,0},{2,3},{3,2},{4,5},{5,4},{6,7},{7,6},{8,9},{9,8},{10,11... | collective-permute-start | bytes 393224 | tf_op jit(solution)/shard_map/ppermute | solution.py:467
  117.2 10.5 %collective-permute-start.25 = (bf16[64,1024]{1,0:T(8,128)(2,1)S(1)}, bf16[64,1024]{1,0:T(8,128)(2,1)S(1)}, u32[]{:S(2)}, u32[]{:S(2)}) collective-permute-start(bf16[64,1024]{1,0:T(8,128)(2,1)S(1)} %get-tuple-element.32), channel_id=1, source_target_pairs={{0,2},{1,3},{2,0},{3,1},{4,6},{5,7},{6,4},{7,5},{8,10},{9,11},{10,... | collective-permute-start | bytes 393224 | tf_op jit(solution)/shard_map/ppermute | solution.py:467
  118.7 9.0 %collective-permute-start.26 = (bf16[64,1024]{1,0:T(8,128)(2,1)S(1)}, bf16[64,1024]{1,0:T(8,128)(2,1)S(1)}, u32[]{:S(2)}, u32[]{:S(2)}) collective-permute-start(bf16[64,1024]{1,0:T(8,128)(2,1)S(1)} %get-tuple-element.33), channel_id=1, source_target_pairs={{0,3},{1,2},{2,1},{3,0},{4,7},{5,6},{6,5},{7,4},{8,11},{9,10},{10,... | collective-permute-start | bytes 393224 | tf_op jit(solution)/shard_map/ppermute | solution.py:467
  126.1 7.8 %collective-permute-start.12 = (bf16[64,1024]{1,0:T(8,128)(2,1)S(1)}, bf16[64,1024]{1,0:T(8,128)(2,1)S(1)}, u32[]{:S(2)}, u32[]{:S(2)}) collective-permute-start(bf16[64,1024]{1,0:T(8,128)(2,1)S(1)} %get-tuple-element.24), channel_id=1, source_target_pairs={{0,2},{1,3},{2,0},{3,1},{4,6},{5,7},{6,4},{7,5},{8,10},{9,11},{10,... | collective-permute-start | bytes 393224 | tf_op jit(solution)/shard_map/ppermute | solution.py:467
  (15 other events, 146.5 us)

commit v2 on v1

v2 whole, which is shorter than its diff:
```python
import functools
import math

import jax
import jax.numpy as jnp
from jax import lax
from jax.experimental import pallas as pl
from jax.experimental.pallas import tpu as pltpu
from jax.sharding import PartitionSpec as P

HEAD = 128
Q = 64
ACC = 8
TENANTS = 4
GROUP = 8
DEAD = -1e30
FOLD = HEAD**-0.5 * math.log2(math.e)
WINDOW = 32
BF = jnp.bfloat16
F32 = jnp.float32
VMEM = pl.BlockSpec(memory_space=pltpu.VMEM)
SMEM = pl.BlockSpec(memory_space=pltpu.SMEM)
ANY = pl.BlockSpec(memory_space=pl.ANY)
HBM = pl.BlockSpec(memory_space=pltpu.HBM)
SMALL = pl.CostEstimate(flops=1, bytes_accessed=1, transcendentals=0)


def limit(mebibytes):
    return pltpu.CompilerParams(vmem_limit_bytes=mebibytes * 1024 * 1024)


def dot(a, b, contract=((1,), (0,))):
    return lax.dot_general(a, b, (contract, ((), ())), preferred_element_type=F32)


def live_devices(tenant, n_seq):
    return max(1, n_seq * 2**tenant // 8)


def live_chips(tenant, n_seq):
    return max(1, live_devices(tenant, n_seq) // 2)


def pieces(x):
    high = x.astype(BF).astype(F32)
    middle = (x - high).astype(BF).astype(F32)
    return high, middle, (x - high - middle).astype(BF).astype(F32)


def stat_tile(columns):
    rows = columns[0].shape[0]
    lane = lax.broadcasted_iota(jnp.int32, (rows, HEAD), 1)
    tile = jnp.zeros((rows, HEAD), F32)
    for h, column in enumerate(columns):
        for k, piece in enumerate(pieces(column)):
            tile = jnp.where(lane == k * GROUP + h, piece, tile)
    return tile.astype(BF)


def reach_kernel(parent_ref, out_ref):
    requests = parent_ref.shape[0]
    row_id = lax.broadcasted_iota(jnp.int32, (2 * Q, 2 * Q), 0)
    column_id = lax.broadcasted_iota(jnp.int32, (2 * Q, 2 * Q), 1)
    chains = []
    for r in range(0, requests, 2):
        up = []
        for k in range(2):
            parent = parent_ref[r + k : r + k + 1, :]
            up.append(jnp.where(parent < 0, -1, parent + k * Q))
        linked = (jnp.concatenate(up, axis=1) == row_id) | (row_id == column_id)
        chains.append(jnp.where(linked, 1.0, 0.0).astype(BF))
    doublings = (Q - 1).bit_length()
    for k in range(doublings):
        contract = ((0,), (1,)) if k == doublings - 1 else ((1,), (0,))
        chains = [jnp.minimum(dot(chain, chain, contract), 1.0).astype(BF) for chain in chains]
    for r in range(requests):
        k = r % 2 * Q
        out_ref[r] = chains[r // 2].astype(F32)[k : k + Q, k : k + Q]


def reach_of(parents):
    return pl.pallas_call(
        reach_kernel,
        out_shape=jax.ShapeDtypeStruct((parents.shape[0], Q, Q), F32),
        in_specs=[VMEM],
        out_specs=VMEM,
        compiler_params=limit(8),
        cost_estimate=SMALL,
        name="reach",
    )(parents)


def attend_kernel(tenant, owners, sources, n_sources, n_after, resident, *refs):
    len_ref, q_ref, kv_ref, reach_ref = refs[:4]
    drafts = refs[4 : 4 + n_sources]
    outs = refs[4 + n_sources + n_after :]
    mine, theirs, copy_ref, len_s, q_s, kv_s, draft_s, m_s, l_s, acc_s, load, store = outs
    count = draft_s.shape[0]
    span = kv_ref.shape[2]
    heads = q_ref.shape[1] // HEAD // 2
    half = heads * HEAD
    rows = heads * Q
    seq = lax.axis_index("seq")
    core = lax.rem(seq, 2)

    def loads(i):
        r = tenant + TENANTS * i
        if resident:
            return []
        return [
            pltpu.make_async_copy(q_ref.at[pl.ds(r * Q, Q), :], q_s.at[i], load.at[i, 0]),
            pltpu.make_async_copy(kv_ref.at[0, r], kv_s.at[i, 0], load.at[i, 1]),
            pltpu.make_async_copy(kv_ref.at[1, r], kv_s.at[i, 1], load.at[i, 2]),
        ]

    def stored(i):
        r = tenant + TENANTS * i
        return pltpu.make_async_copy(kv_ref.at[:, r] if resident else kv_s.at[i], copy_ref.at[:, r], store.at[i])

    def cached(i, x, columns):
        return kv_ref[x, tenant + TENANTS * i, :, columns] if resident else kv_s[i, x, :, columns]

    small = [pltpu.make_async_copy(len_ref, len_s, load.at[count, 0])]
    given = [pltpu.make_async_copy(drafts[sources[i]], draft_s.at[i], load.at[i, 3]) for i in range(count)]
    for copy in (*loads(0), *small, *[c for i in range(1, count) for c in loads(i)], *given):
        copy.start()
    for copy in small:
        copy.wait()

    def columns_of(g):
        kv = g * heads // GROUP
        return slice(kv * HEAD, (kv + 1) * HEAD)

    for i in range(count):
        r = tenant + TENANTS * i
        alive = len_s[r] - seq * span
        for copy in loads(i):
            copy.wait()
        given[i].wait()
        stored(i).start()

        def queries_of(g):
            held = q_ref.at[pl.ds(r * Q, Q)] if resident else q_s.at[i]
            return jnp.concatenate(
                [held[:, (g * heads + h) * HEAD : (g * heads + h + 1) * HEAD] for h in range(heads)], axis=0
            )

        @pl.when(alive > 0)
        def _():
            keep = lax.broadcasted_iota(jnp.int32, (span, HEAD), 0) < alive
            ones = jnp.where(keep, 1.0, 0.0).astype(BF)

            def scores(g):
                keys = cached(i, 0, columns_of(g))
                keys = jnp.where(keep, keys, jnp.broadcast_to(keys[:1], keys.shape))
                return dot(queries_of(g), keys, ((1,), (1,)))

            def weigh(g, m, w):
                values = cached(i, 1, columns_of(g))
                values = jnp.where(keep, values, jnp.zeros_like(values))
                o = dot(w, jnp.concatenate([values, ones], axis=1))
                place = slice(g * rows, (g + 1) * rows)
                m_s[place] = jnp.broadcast_to(m, (rows, HEAD))
                acc_s[place] = o[:, :HEAD]
                l_s[place] = o[:, HEAD:]

            upcoming = scores(0)
            pending = None
            for g in range(2):
                s = upcoming
                if g == 0:
                    upcoming = scores(1)
                m = jnp.max(s, axis=1, keepdims=True) * FOLD
                w = jnp.exp2(s * FOLD - m).astype(BF)
                if pending is not None:
                    weigh(*pending)
                pending = (g, m, w)
            weigh(*pending)

        @pl.when(alive <= 0)
        def _():
            m_s[...] = jnp.full_like(m_s, DEAD)
            l_s[...] = jnp.zeros_like(l_s)
            acc_s[...] = jnp.zeros_like(acc_s)

        @pl.when(seq == owners[i])
        def _():
            reach = jnp.concatenate([reach_ref[r]] * heads, axis=0) > 0.5
            for g in range(2):
                place = slice(g * rows, (g + 1) * rows)
                s = dot(queries_of(g), draft_s[i, 0, :, columns_of(g)], ((1,), (1,)))
                s = jnp.where(reach, s, DEAD)
                m_old = m_s[place]
                m = jnp.maximum(m_old, jnp.max(s, axis=1, keepdims=True) * FOLD)
                w = jnp.exp2(s * FOLD - m[:, :Q])
                shrink = jnp.exp2(m_old - m)
                l_s[place] = l_s[place] * shrink + jnp.sum(w, axis=1, keepdims=True)
                m_s[place] = m
                acc_s[place] = acc_s[place] * shrink + dot(w.astype(BF), draft_s[i, 1, :, columns_of(g)])

        def finish(g, out):
            stats = []
            for h in range(heads):
                place = slice((g * heads + h) * Q, (g * heads + h + 1) * Q)
                total = l_s[place]
                some = total > 0.0
                total = jnp.where(some, total, 1.0)
                out[i * Q : (i + 1) * Q, h * HEAD : (h + 1) * HEAD] = (acc_s[place] / total).astype(BF)
                stats.append(jnp.where(some, m_s[place] + jnp.log2(total), DEAD))
            out[i * Q : (i + 1) * Q, half:] = stat_tile(stats)

        for g in range(2):

            @pl.when(core == g)
            def _():
                finish(g, mine)
                finish(1 - g, theirs)

    for i in range(count):
        stored(i).wait()


def attend(tenant, queries, cache, reach, lengths, drafts, owners, sources, copy, after, resident=False):
    requests, span = cache.shape[1], cache.shape[2]
    count = requests // TENANTS
    used = sorted(set(sources))
    width, kv_width = queries.shape[1], cache.shape[3]
    wide = width // 2 + HEAD
    out = jax.ShapeDtypeStruct((count * Q, wide), BF)
    carried = [] if copy is None else [copy]
    extra = list(after) + carried
    return pl.pallas_call(
        functools.partial(attend_kernel, tenant, owners, [used.index(s) for s in sources], len(used), len(extra), resident),
        in_specs=[HBM] + [VMEM if resident else HBM] * 2 + [VMEM] + [HBM] * len(used) + [ANY] * len(extra),
        out_specs=[VMEM, VMEM, ANY],
        scratch_shapes=[
            pltpu.SMEM((requests,), jnp.int32),
            pltpu.VMEM((1 if resident else count, Q, width), BF),
            pltpu.VMEM((1, 1, 16, HEAD) if resident else (count, 2, span, kv_width), BF),
            pltpu.VMEM((count, 2, Q, kv_width), BF),
            pltpu.VMEM((Q * width // HEAD, HEAD), F32),
            pltpu.VMEM((Q * width // HEAD, HEAD), F32),
            pltpu.VMEM((Q * width // HEAD, HEAD), F32),
            pltpu.SemaphoreType.DMA((count + 1, 4)),
            pltpu.SemaphoreType.DMA((count,)),
        ],
        out_shape=[out, out, jax.ShapeDtypeStruct(cache.shape, BF)],
        input_output_aliases={3 + len(used) + len(extra): 2} if carried else {},
        compiler_params=limit(28),
        cost_estimate=SMALL,
        name=f"attend_{tenant}",
    )(lengths, queries, cache, reach, *[drafts[s] for s in used], *extra)


def combine_kernel(final, a_ref, b_ref, *rest):
    out_ref = rest[-1]
    rows = a_ref.shape[0]
    half = a_ref.shape[1] - HEAD
    heads = half // HEAD

    def stats_of(ref):
        tile = ref[:, half:].astype(F32)
        return tile[:, :GROUP] + tile[:, GROUP : 2 * GROUP] + tile[:, 2 * GROUP : 3 * GROUP]

    a, b = stats_of(a_ref), stats_of(b_ref)
    top = jnp.maximum(a, b)
    weight_a, weight_b = jnp.exp2(a - top), jnp.exp2(b - top)
    total = weight_a + weight_b
    weight_a, weight_b = weight_a / total, weight_b / total
    level = top + jnp.log2(total)
    for h in range(heads):
        place = slice(h * HEAD, (h + 1) * HEAD)
        out_ref[:, place] = (
            a_ref[:, place].astype(F32) * weight_a[:, h : h + 1]
            + b_ref[:, place].astype(F32) * weight_b[:, h : h + 1]
        ).astype(BF)
    if not final:
        out_ref[:, half:] = stat_tile(
            [jnp.broadcast_to(level[:, h : h + 1], (rows, HEAD)) for h in range(heads)]
        )


def combine(a, b, final, after=()):
    rows, wide = a.shape
    return pl.pallas_call(
        functools.partial(combine_kernel, final),
        out_shape=jax.ShapeDtypeStruct((rows, wide - HEAD if final else wide), BF),
        in_specs=[VMEM, VMEM] + [ANY for _ in after],
        out_specs=VMEM,
        compiler_params=limit(8),
        cost_estimate=SMALL,
        name="combine",
    )(a, b, *after)


def project_kernel(requests, n_tp, tenants, n_after, *refs):
    count = len(tenants)
    parts = refs[: 2 * count]
    w_ref = refs[2 * count]
    own_ref, *outs = refs[2 * count + 1 + n_after : -1]
    product = refs[-1]
    tp = lax.axis_index("tp")
    core = lax.rem(lax.axis_index("seq"), 2)
    half = w_ref.shape[0] // 2
    mine = jnp.concatenate([parts[2 * k][...] for k in range(count)], axis=0)
    other = jnp.concatenate([parts[2 * k + 1][...] for k in range(count)], axis=0)
    near = pl.ds(pl.multiple_of(core * half, half), half)
    far = pl.ds(pl.multiple_of((1 - core) * half, half), half)
    product[...] = dot(mine, w_ref[near, :]) + dot(other, w_ref[far, :])
    each = requests // TENANTS
    share = requests // n_tp
    taken = {}
    for k, tenant in enumerate(tenants):
        for i in range(each):
            r = tenant + TENANTS * i
            taken.setdefault(r // share, []).append((r % share, k * each + i))
    for owner in range(n_tp):
        for slot in range(n_tp):

            @pl.when((owner ^ tp) == slot)
            def _():
                for place, (_, block) in enumerate(sorted(taken[owner])):
                    value = product[block * Q : (block + 1) * Q, :]
                    target = own_ref if slot == 0 else outs[slot - 1]
                    target[place * Q : (place + 1) * Q, :] = value.astype(target.dtype)


def project(requests, n_tp, tenants, parts, weight, after):
    depth, columns = weight.shape
    rows = len(tenants) * (requests // TENANTS) * Q
    mine = rows // n_tp
    return pl.pallas_call(
        functools.partial(project_kernel, requests, n_tp, tenants, len(after)),
        in_specs=[VMEM] * (len(parts) + 1) + [ANY] * len(after),
        out_specs=[VMEM] * n_tp,
        out_shape=[jax.ShapeDtypeStruct((mine, columns), F32)]
        + [jax.ShapeDtypeStruct((mine, columns), BF)] * (n_tp - 1),
        scratch_shapes=[pltpu.VMEM((rows, columns), F32)],
        compiler_params=limit(20),
        cost_estimate=SMALL,
        name="project",
    )(*parts, weight, *after)


def pick_kernel(n_tokens, first, last, *refs):
    out_ref = refs[-1]
    value, *others = refs[: len(refs) - 1 - n_tokens]
    chip = lax.axis_index("seq") // 2
    inside = (chip >= first) & (chip <= last)

    @pl.when(inside)
    def _():
        out_ref[...] = value[...]

    @pl.when(jnp.logical_not(inside))
    def _():
        out_ref[...] = functools.reduce(jnp.add, [other[...] for other in others])


def pick(value, others, first, last, after):
    return pl.pallas_call(
        functools.partial(pick_kernel, len(after), first, last),
        out_shape=jax.ShapeDtypeStruct(value.shape, BF),
        in_specs=[VMEM] * (1 + len(others)) + [ANY] * len(after),
        out_specs=VMEM,
        compiler_params=limit(8),
        cost_estimate=SMALL,
        name="pick",
    )(value, *others, *after)


def stack_kernel(a_ref, b_ref, *rest):
    out_ref = rest[-1]
    size = a_ref.shape[0]
    out_ref[:size] = a_ref[...]
    out_ref[size:] = b_ref[...]


def stack(a, b, after):
    return pl.pallas_call(
        stack_kernel,
        out_shape=jax.ShapeDtypeStruct((2 * a.shape[0], *a.shape[1:]), BF),
        in_specs=[VMEM, VMEM] + [ANY] * len(after),
        out_specs=VMEM,
        compiler_params=limit(4),
        cost_estimate=SMALL,
        name="stack",
    )(a, b, *after)


def choose_kernel(path_ref, draft_ref, out_ref):
    seq = lax.axis_index("seq")
    row = lax.broadcasted_iota(jnp.int32, (ACC, Q), 0)
    column = lax.broadcasted_iota(jnp.int32, (ACC, Q), 1)
    picked = jnp.zeros((ACC, Q), jnp.int32)
    for j in range(ACC):
        picked = jnp.where(row == j, path_ref[seq, j], picked)
    selector = jnp.where(picked == column, 1.0, 0.0).astype(BF)
    for x in range(2):
        out_ref[0, x] = dot(selector, draft_ref[x]).astype(BF)


def choose(path, draft_kv):
    return pl.pallas_call(
        choose_kernel,
        out_shape=jax.ShapeDtypeStruct((1, 2, ACC, draft_kv.shape[2]), BF),
        in_specs=[SMEM, VMEM],
        out_specs=VMEM,
        compiler_params=limit(4),
        name="choose",
    )(path, draft_kv)


def patch_kernel(len_ref, accept_ref, cache_ref, chosen_ref, out_ref, window, load_sem, store_sem):
    requests, span = cache_ref.shape[1], cache_ref.shape[2]
    seq = lax.axis_index("seq")

    def place_of(r):
        first = len_ref[r] - seq * span
        start = jnp.clip(first // 16 * 16, 0, span - WINDOW)
        return first, pl.multiple_of(start, 16), (first + ACC > 0) & (first < span)

    def load(r):
        _, start, here = place_of(r)
        return here, pltpu.make_async_copy(
            cache_ref.at[:, r, pl.ds(start, WINDOW), :], window.at[r], load_sem.at[r]
        )

    def store(r):
        _, start, here = place_of(r)
        return here, pltpu.make_async_copy(
            window.at[r], out_ref.at[:, r, pl.ds(start, WINDOW), :], store_sem.at[r]
        )

    for r in range(requests):
        here, copy = load(r)
        pl.when(here)(copy.start)
    for r in range(requests):
        here, copy = load(r)
        first, start, _ = place_of(r)

        @pl.when(here)
        def _():
            copy.wait()
            row = lax.broadcasted_iota(jnp.int32, window.shape[2:], 0) + (start - first)
            for x in range(2):
                value = window[r, x].astype(F32)
                rows = chosen_ref[r ^ seq, x].astype(F32)
                for j in range(ACC):
                    value = jnp.where((row == j) & (j < accept_ref[r]), rows[j : j + 1], value)
                window[r, x] = value.astype(BF)
            store(r)[1].start()

    for r in range(requests):
        here, copy = store(r)
        pl.when(here)(copy.wait)


def patched(cache, chosen, lengths, accepted):
    requests = cache.shape[1]
    return pl.pallas_call(
        patch_kernel,
        out_shape=jax.ShapeDtypeStruct(cache.shape, BF),
        in_specs=[SMEM, SMEM, ANY, VMEM],
        out_specs=ANY,
        scratch_shapes=[
            pltpu.VMEM((requests, 2, WINDOW, cache.shape[3]), BF),
            pltpu.SemaphoreType.DMA((requests,)),
            pltpu.SemaphoreType.DMA((requests,)),
        ],
        input_output_aliases={2: 0},
        compiler_params=limit(8),
        name="patch_cache",
    )(lengths, accepted, cache, chosen)


def chip_pairs(pairs):
    return [(2 * a + c, 2 * b + c) for a, b in pairs for c in range(2)]


def local(n_seq, n_tp, queries, cache, draft_kv, out_weight, lengths, parents, path, accepted):
    requests = cache.shape[1]
    chips = n_seq // 2
    seq = lax.axis_index("seq")
    chip = seq // 2
    swap_pairs = [(s, s ^ 1) for s in range(n_seq)]

    def swap(array):
        return lax.ppermute(array, "seq", swap_pairs)

    def send(array, pairs):
        return lax.ppermute(array, "seq", chip_pairs(pairs))

    owners, sources, rounds = {}, {}, []
    for r in range(requests):
        owners[r] = r % live_devices(r % TENANTS, n_seq)
        sources[r] = 0
        if owners[r] != r:
            for k, taken in enumerate(rounds):
                if all(owners[r] != b for _, b in taken):
                    break
            else:
                k = len(rounds)
                rounds.append([])
            rounds[k].append((r, owners[r]))
            sources[r] = k + 1
    drafts = [draft_kv] + [lax.ppermute(draft_kv, "seq", pairs) for pairs in rounds]

    copy = None

    reach = reach_of(parents)

    def partial_of(tenant, after=()):
        nonlocal copy
        own = range(tenant, requests, TENANTS)
        mine, theirs, copy = attend(
            tenant,
            queries,
            cache,
            reach,
            lengths,
            drafts,
            [owners[r] for r in own],
            [sources[r] for r in own],
            copy,
            list(after),
            resident=tenant != 3,
        )
        return mine, swap(theirs)

    count = {tenant: live_chips(tenant, n_seq) for tenant in range(TENANTS)}
    steps, value = {}, {}
    for tenant in range(TENANTS):
        last, half = count[tenant] - 1, count[tenant] // 2
        steps[tenant] = [[(k, k + 1), (last - k, last - k - 1)] for k in range(half)]

    def join(tenant, pair, after=()):
        value[tenant] = combine(*pair, count[tenant] == 1, after)

    def advance(tenant, after=()):
        if steps[tenant]:
            arrived = send(value[tenant], steps[tenant].pop(0))
            value[tenant] = combine(value[tenant], arrived, not steps[tenant], after)

    def spread(tenant, after=()):
        first = max(count[tenant] // 2 - 1, 0)
        last = count[tenant] // 2
        inside = (chip >= first) & (chip <= last)
        top = (first, last)
        newest = value[tenant]
        if chips == 4 and last == 0:
            newest = send(newest, [(0, 2)])
            held = [newest, send(newest, [(2, 1)]), send(newest, [(2, 3)])]
        else:
            held = []
            while first > 0 or last < chips - 1:
                pairs = []
                if first > 0:
                    pairs.append((first, first - 1))
                    first -= 1
                if last < chips - 1:
                    pairs.append((last, last + 1))
                    last += 1
                newest = send(newest, pairs)
                held.append(newest)
        if held and after:
            value[tenant] = pick(value[tenant], held, top[0], top[1], after)
        elif held:
            value[tenant] = jnp.where(inside, value[tenant], functools.reduce(jnp.add, held))

    join(3, partial_of(3))
    zero = partial_of(0, [value[3]])
    advance(3, [zero[0]])
    join(0, zero, [value[3]])
    two = partial_of(2, [value[0]])
    join(2, two)
    one = partial_of(1, [value[2]])
    advance(3, [one[0]])
    advance(2, [value[3]])
    join(1, one, [value[2]])
    whole = {}
    for tenant in (3, 0, 2, 1):
        while steps[tenant]:
            advance(tenant, [value[1]])

    def sums(tenants, after):
        parts = [part for tenant in tenants for part in whole[tenant]]
        own, *others = project(requests, n_tp, tenants, parts, out_weight, after)
        arrived = [
            lax.ppermute(other, "tp", [(t, t ^ (k + 1)) for t in range(n_tp)]).astype(F32)
            for k, other in enumerate(others)
        ]
        return own, functools.reduce(jnp.add, arrived, own).astype(BF)

    for tenant in (3, 0):
        spread(tenant)
        whole[tenant] = (value[tenant], swap(value[tenant]))
    own, one_sum = sums((3, 0), [])
    for tenant in (2, 1):
        spread(tenant, [own])
        whole[tenant] = (value[tenant], swap(value[tenant]))
    _, other_sum = sums((2, 1), [one_sum])

    assert requests == 2 * n_tp
    even = lax.axis_index("tp") % 2 == 0
    attn_out = jnp.concatenate(
        [jnp.where(even, one_sum, other_sum), jnp.where(even, other_sum, one_sum)], axis=0
    )

    chosen = choose(path, draft_kv)
    distance = 1
    while distance < n_seq:
        arrived = lax.ppermute(chosen, "seq", [(s, s ^ distance) for s in range(n_seq)])
        chosen = jnp.concatenate([chosen, arrived], axis=0)
        distance *= 2
    new_cache = patched(copy, chosen, lengths, accepted)
    return attn_out, new_cache


def solution(mesh):
    return jax.shard_map(
        functools.partial(local, mesh.shape["seq"], mesh.shape["tp"]),
        mesh=mesh,
        in_specs=(
            P(None, "tp"),
            P(None, None, "seq", "tp"),
            P(None, "seq", "tp"),
            P("tp", "seq"),
            P(),
            P(),
            P(),
            P(),
        ),
        out_specs=(P("tp", "seq"), P(None, None, "seq", "tp")),
        check_vma=False,
    )
```

time: 135 us -> 97.9 us (0.73)
  Pallas kernels: 57.7 us -> 30 us
  waiting for transfers between devices: 35.4 us -> 12.3 us
  starting transfers between devices: 33.5 us -> 43.5 us
  local copies, waits for them, and re-layouts: 5.98 us -> 9.36 us
    ppermute x12, waiting for transfers between devices: 22.7 us -> 4.94 us  [send(): return lax.ppermute(array, 'seq', chip_pairs(pairs))]
    pallas_call x4, Pallas kernels: 36 us -> 19.3 us  [attend(): pl.pallas_call(functools.partial(attend_kernel, tenant, owners, [used.ind...]
    pallas_call x3 -> x5, Pallas kernels: 14.6 us -> 3.89 us  [the longest x2 2.72 us: project(): pl.pallas_call(functools.partial(project_kernel, requests, n_tp, tenants,...]
    ppermute x12, starting transfers between devices: 12 us -> 21.8 us  [send(): return lax.ppermute(array, 'seq', chip_pairs(pairs))]
    ppermute x1, waiting for transfers between devices: 6.47 us -> 0.64 us  [local(): lax.ppermute(draft_kv, 'seq', pairs)]
    unnamed x18 -> x22, local copies, waits for them, and re-layouts: 5.98 us -> 9.36 us
    ppermute x6, waiting for transfers between devices: 6.17 us -> 4.31 us  [sums(): lax.ppermute(other, 'tp', [(t, t ^ k + 1) for t in range(n_tp)]).astype(F32)]
    ppermute x3, waiting for transfers between devices: 0.01 us -> 1.56 us  [local(): lax.ppermute(chosen, 'seq', [(s, s ^ distance) for s in range(n_seq)])]
  transfers between devices with their start and end apart: 30 -> 30, of which waited for: 8 -> 7; matrix products, arithmetic and copies ran while one was open for 0% -> 0% of each run, Pallas kernels for 37% -> 20%
where the time goes in v2:
time: 97.9 us; the launch traced here: 97.3 us
  starting transfers between devices  43.5 us (44%)
  Pallas kernels  30 us (31%)
  waiting for transfers between devices  12.3 us (13%)
  local copies, waits for them, and re-layouts  9.36 us (10%)
  between operations  1.15 us (1%)
  other arithmetic  1.01 us (1%)
    ppermute x12, starting transfers between devices, send(): return lax.ppermute(array, 'seq', chip_pairs(pairs))  21.8 us
    pallas_call x4, Pallas kernels, attend(): pl.pallas_call(functools.partial(attend_kernel, tenant, owners, [used.ind...  19.3 us
    ppermute x3, starting transfers between devices, local(): lax.ppermute(chosen, 'seq', [(s, s ^ distance) for s in range(n_seq)])  10.4 us
    unnamed x22, local copies, waits for them, and re-layouts  9.36 us
    ppermute x6, starting transfers between devices, sums(): lax.ppermute(other, 'tp', [(t, t ^ k + 1) for t in range(n_tp)]).astype(F32)  7.35 us
    ppermute x12, waiting for transfers between devices, send(): return lax.ppermute(array, 'seq', chip_pairs(pairs))  4.94 us
    ppermute x6, waiting for transfers between devices, sums(): lax.ppermute(other, 'tp', [(t, t ^ k + 1) for t in range(n_tp)]).astype(F32)  4.31 us
    pallas_call x7, Pallas kernels, combine(): pl.pallas_call(functools.partial(combine_kernel, final), out_shape=jax.Sh...  3.85 us
  transfers between devices with their start and end apart: 30, of which 7 were waited for; matrix products, arithmetic and copies ran while one was open for 0% of the time, Pallas kernels for 20%

profile of v2, /device:TPU:0, one launch (start us, length us, event | category | flops | bytes accessed | tf_op | source)
XLA Modules:
  0.0 97.3 jit_solution(4348446726242720785)
XLA Ops:
  2.5 3.4 %copy-done = bf16[2,8,1024,256]{3,2,1,0:T(8,128)(2,1)S(1)} copy-done((bf16[2,8,1024,256]{3,2,1,0:T(8,128)(2,1)S(1)}, bf16[2,8,1024,256]{3,2,1,0:T(8,128)(2,1)}, u32[]{:S(2)}) %copy-start) | copy-done | bytes 8388632
  5.8 1.6 %copy-done.1 = bf16[512,2048]{1,0:T(8,128)(2,1)S(1)} copy-done((bf16[512,2048]{1,0:T(8,128)(2,1)S(1)}, bf16[512,2048]{1,0:T(8,128)(2,1)}, u32[]{:S(2)}) %copy-start.1) | copy-done | bytes 2097176
  8.9 4.4 %attend_3.1 = (bf16[128,1152]{1,0:T(8,128)(2,1)S(1)}, bf16[128,1152]{1,0:T(8,128)(2,1)S(1)}, bf16[2,8,1024,256]{3,2,1,0:T(8,128)(2,1)}) custom-call(s32[8]{0:T(128)S(1)} %copy-done.6, bf16[512,2048]{1,0:T(8,128)(2,1)S(1)} %copy-done.1, bf16[2,8,1024,256]{3,2,1,0:T(8,128)(2,1)S(1)} %copy-done, f32[8,64,64]{2,1,0:T(8,128)S(1)} %reach.1.refs_3_, ...), custom_call_target="tpu_custom_call" | custom-call | flops 1 | bytes 1 | tf_op jit(solution)/shard_map/attend_3/pallas_call | solution.py:232
  15.8 5.0 %collective-permute-start.1 = (bf16[128,1152]{1,0:T(8,128)(2,1)S(1)}, bf16[128,1152]{1,0:T(8,128)(2,1)S(1)}, u32[]{:S(2)}, u32[]{:S(2)}) collective-permute-start(bf16[128,1152]{1,0:T(8,128)(2,1)S(1)} %combine.7.refs_6_.a_ref), channel_id=1, source_target_pairs={{0,8},{4,12},{24,16},{28,20},{1,9},{5,13},{25,17},{29,21},{2,10},{... | collective-permute-start | bytes 884744 | tf_op jit(solution)/shard_map/ppermute | solution.py:492
  21.5 5.9 %attend_0.1 = (bf16[128,1152]{1,0:T(8,128)(2,1)S(1)}, bf16[128,1152]{1,0:T(8,128)(2,1)S(1)}, bf16[2,8,1024,256]{3,2,1,0:T(8,128)(2,1)}) custom-call(s32[8]{0:T(128)S(1)} %copy-done.7, bf16[512,2048]{1,0:T(8,128)(2,1)S(1)} %copy-done.1, bf16[2,8,1024,256]{3,2,1,0:T(8,128)(2,1)S(1)} %copy-done, ...), custom_call_target="tpu_custom_call", output_to_operand_aliasing={{2}: (7, {})} | custom-call | flops 1 | bytes 1 | tf_op jit(solution)/shard_map/attend_0/pallas_call | solution.py:232
  29.5 4.4 %attend_2.1 = (bf16[128,1152]{1,0:T(8,128)(2,1)S(1)}, bf16[128,1152]{1,0:T(8,128)(2,1)S(1)}, bf16[2,8,1024,256]{3,2,1,0:T(8,128)(2,1)}) custom-call(s32[8]{0:T(128)S(1)} %copy-done.7, bf16[512,2048]{1,0:T(8,128)(2,1)S(1)} %copy-done.1, bf16[2,8,1024,256]{3,2,1,0:T(8,128)(2,1)S(1)} %copy-done, ...), custom_call_target="tpu_custom_call", output_to_operand_aliasing={{2}: (7, {})} | custom-call | flops 1 | bytes 1 | tf_op jit(solution)/shard_map/attend_2/pallas_call | solution.py:232
  34.1 1.9 %collective-permute-start.8 = (bf16[128,1024]{1,0:T(8,128)(2,1)S(1)}, bf16[128,1024]{1,0:T(8,128)(2,1)S(1)}, u32[]{:S(2)}, u32[]{:S(2)}) collective-permute-start(bf16[128,1024]{1,0:T(8,128)(2,1)S(1)} %combine.9.refs_6_), channel_id=1, source_target_pairs={{0,16},{4,20},{1,17},{5,21},{2,18},{6,22},{3,19},{7,23}} | collective-permute-start | bytes 786440 | tf_op jit(solution)/shard_map/ppermute | solution.py:492
  37.3 4.8 %collective-permute-start.15 = (bf16[128,1152]{1,0:T(8,128)(2,1)S(1)}, bf16[128,1152]{1,0:T(8,128)(2,1)S(1)}, u32[]{:S(2)}, u32[]{:S(2)}) collective-permute-start(bf16[128,1152]{1,0:T(8,128)(2,1)S(1)} %combine.10.refs_6_.a_ref), channel_id=1, source_target_pairs={{0,8},{4,12},{8,0},{12,4},{1,9},{5,13},{9,1},{13,5},{2,10},{6,14},... | collective-permute-start | bytes 884744 | tf_op jit(solution)/shard_map/ppermute | solution.py:492
  42.2 4.6 %attend_1.1 = (bf16[128,1152]{1,0:T(8,128)(2,1)S(1)}, bf16[128,1152]{1,0:T(8,128)(2,1)S(1)}, bf16[2,8,1024,256]{3,2,1,0:T(8,128)(2,1)}) custom-call(s32[8]{0:T(128)S(1)} %copy-done.7, bf16[512,2048]{1,0:T(8,128)(2,1)S(1)} %copy-done.1, bf16[2,8,1024,256]{3,2,1,0:T(8,128)(2,1)S(1)} %copy-done, ...), custom_call_target="tpu_custom_call", output_to_operand_aliasing={{2}: (7, {})} | custom-call | flops 1 | bytes 1 | tf_op jit(solution)/shard_map/attend_1/pallas_call | solution.py:232
  46.8 1.6 %collective-permute-start.19 = (bf16[128,1152]{1,0:T(8,128)(2,1)S(1)}, bf16[128,1152]{1,0:T(8,128)(2,1)S(1)}, u32[]{:S(2)}, u32[]{:S(2)}) collective-permute-start(bf16[128,1152]{1,0:T(8,128)(2,1)S(1)} %get-tuple-element.36), channel_id=1, source_target_pairs={{0,4},{4,0},{8,12},{12,8},{16,20},{20,16},{24,28},{28,24},{1,5},{5... | collective-permute-start | bytes 884744 | tf_op jit(solution)/shard_map/ppermute | solution.py:489
  52.6 4.1 %collective-permute-start.20 = (bf16[128,1024]{1,0:T(8,128)(2,1)S(1)}, bf16[128,1024]{1,0:T(8,128)(2,1)S(1)}, u32[]{:S(2)}, u32[]{:S(2)}) collective-permute-start(bf16[128,1024]{1,0:T(8,128)(2,1)S(1)} %combine.13.refs_0_), channel_id=1, source_target_pairs={{0,16},{4,20},{1,17},{5,21},{2,18},{6,22},{3,19},{7,23}} | collective-permute-start | bytes 786440 | tf_op jit(solution)/shard_map/ppermute | solution.py:492
  57.6 2.8 %collective-permute-done.6 = bf16[128,1024]{1,0:T(8,128)(2,1)S(1)} collective-permute-done((bf16[128,1024]{1,0:T(8,128)(2,1)S(1)}, bf16[128,1024]{1,0:T(8,128)(2,1)S(1)}, u32[]{:S(2)}, u32[]{:S(2)}) %collective-permute-start.6) | collective-permute-done | bytes 262176 | tf_op jit(solution)/shard_map/ppermute | solution.py:492
  60.5 2.0 %collective-permute-done.20.refs_1_ = bf16[128,1024]{1,0:T(8,128)(2,1)S(1)} collective-permute-done((bf16[128,1024]{1,0:T(8,128)(2,1)S(1)}, bf16[128,1024]{1,0:T(8,128)(2,1)S(1)}, u32[]{:S(2)}, u32[]{:S(2)}) %collective-permute-start.20) | collective-permute-done | bytes 262176 | tf_op jit(solution)/shard_map/ppermute | solution.py:492
  65.4 2.2 %copy-done.2 = bf16[2048,1024]{1,0:T(8,128)(2,1)S(1)} copy-done((bf16[2048,1024]{1,0:T(8,128)(2,1)S(1)}, bf16[2048,1024]{1,0:T(8,128)(2,1)}, u32[]{:S(2)}) %copy-start.2) | copy-done | bytes 4194328
  68.9 2.2 %collective-permute-start.12 = (bf16[64,1024]{1,0:T(8,128)(2,1)S(1)}, bf16[64,1024]{1,0:T(8,128)(2,1)S(1)}, u32[]{:S(2)}, u32[]{:S(2)}) collective-permute-start(bf16[64,1024]{1,0:T(8,128)(2,1)S(1)} %get-tuple-element.33), channel_id=1, source_target_pairs={{0,1},{1,0},{2,3},{3,2},{4,5},{5,4},{6,7},{7,6},{8,9},{9,8},{10,11... | collective-permute-start | bytes 393224 | tf_op jit(solution)/shard_map/ppermute | solution.py:590
  71.2 1.5 %collective-permute-start.13 = (bf16[64,1024]{1,0:T(8,128)(2,1)S(1)}, bf16[64,1024]{1,0:T(8,128)(2,1)S(1)}, u32[]{:S(2)}, u32[]{:S(2)}) collective-permute-start(bf16[64,1024]{1,0:T(8,128)(2,1)S(1)} %get-tuple-element.34), channel_id=1, source_target_pairs={{0,2},{1,3},{2,0},{3,1},{4,6},{5,7},{6,4},{7,5},{8,10},{9,11},{10,... | collective-permute-start | bytes 393224 | tf_op jit(solution)/shard_map/ppermute | solution.py:590
  72.7 5.8 %collective-permute-start.28 = (bf16[2,2,8,256]{3,2,1,0:T(8,128)(2,1)S(1)}, bf16[2,2,8,256]{3,2,1,0:T(8,128)(2,1)S(1)}, u32[]{:S(2)}, u32[]{:S(2)}) collective-permute-start(bf16[2,2,8,256]{3,2,1,0:T(8,128)(2,1)S(1)} %pad_maximum_fusion.3), channel_id=1, source_target_pairs={{0,8},{4,12},{8,0},{12,4},{16,24},{20,28},{24,16},{28,20},{1,9},{5... | collective-permute-start | bytes 49160 | tf_op jit(solution)/shard_map/ppermute | solution.py:613
  78.6 1.6 %collective-permute-done.28 = bf16[2,2,8,256]{3,2,1,0:T(8,128)(2,1)S(1)} collective-permute-done((bf16[2,2,8,256]{3,2,1,0:T(8,128)(2,1)S(1)}, bf16[2,2,8,256]{3,2,1,0:T(8,128)(2,1)S(1)}, u32[]{:S(2)}, u32[]{:S(2)}) %collective-permute-start.28) | collective-permute-done | bytes 16416 | tf_op jit(solution)/shard_map/ppermute | solution.py:613
  80.2 4.6 %collective-permute-start.29 = (bf16[4,2,8,256]{3,2,1,0:T(8,128)(2,1)S(1)}, bf16[4,2,8,256]{3,2,1,0:T(8,128)(2,1)S(1)}, u32[]{:S(2)}, u32[]{:S(2)}) collective-permute-start(bf16[4,2,8,256]{3,2,1,0:T(8,128)(2,1)S(1)} %pad_maximum_fusion.2), channel_id=1, source_target_pairs={{0,16},{4,20},{8,24},{12,28},{16,0},{20,4},{24,8},{28,12},{1,17},{... | collective-permute-start | bytes 98312 | tf_op jit(solution)/shard_map/ppermute | solution.py:613
  85.0 1.4 %project.3 = (f32[64,1024]{1,0:T(8,128)S(1)}, bf16[64,1024]{1,0:T(8,128)(2,1)S(1)}, bf16[64,1024]{1,0:T(8,128)(2,1)S(1)}, bf16[64,1024]{1,0:T(8,128)(2,1)S(1)}) custom-call(bf16[128,1024]{1,0:T(8,128)(2,1)S(1)} %pick.2.refs_0_, bf16[128,1024]{1,0:T(8,128)(2,1)S(1)} %collective-permute-done.18.refs_1_, bf16[128,1024]{1,0:T(8,128)(2,1)S(1)} %pick.3.refs_2_, ...), custom_call_target="tpu_custom_call" | custom-call | flops 1 | bytes 1 | tf_op jit(solution)/shard_map/project/pallas_call | solution.py:332
  86.3 2.0 %collective-permute-start.24 = (bf16[64,1024]{1,0:T(8,128)(2,1)S(1)}, bf16[64,1024]{1,0:T(8,128)(2,1)S(1)}, u32[]{:S(2)}, u32[]{:S(2)}) collective-permute-start(bf16[64,1024]{1,0:T(8,128)(2,1)S(1)} %get-tuple-element.38), channel_id=1, source_target_pairs={{0,1},{1,0},{2,3},{3,2},{4,5},{5,4},{6,7},{7,6},{8,9},{9,8},{10,11... | collective-permute-start | bytes 393224 | tf_op jit(solution)/shard_map/ppermute | solution.py:590
  88.3 1.5 %collective-permute-start.25 = (bf16[64,1024]{1,0:T(8,128)(2,1)S(1)}, bf16[64,1024]{1,0:T(8,128)(2,1)S(1)}, u32[]{:S(2)}, u32[]{:S(2)}) collective-permute-start(bf16[64,1024]{1,0:T(8,128)(2,1)S(1)} %get-tuple-element.39), channel_id=1, source_target_pairs={{0,2},{1,3},{2,0},{3,1},{4,6},{5,7},{6,4},{7,5},{8,10},{9,11},{10,... | collective-permute-start | bytes 393224 | tf_op jit(solution)/shard_map/ppermute | solution.py:590
  89.9 2.2 %patch_cache.1 = bf16[2,8,1024,256]{3,2,1,0:T(8,128)(2,1)} custom-call(s32[8]{0:T(128)S(1)} %copy-done.7, s32[8]{0:T(128)S(1)} %copy-done.10, bf16[2,8,1024,256]{3,2,1,0:T(8,128)(2,1)} %get-tuple-element.41.cache_ref, bf16[8,2,8,256]{3,2,1,0:T(8,128)(2,1)S(1)} %pad_maximum_fusion.1.chosen_ref), custom_call_target="tpu_custom_call", output_to_operand_aliasing={{}: (2, {})} | custom-call | tf_op jit(solution)/shard_map/patch_cache/pallas_call | solution.py:461
  92.3 4.2 %collective-permute-done.25 = bf16[64,1024]{1,0:T(8,128)(2,1)S(1)} collective-permute-done((bf16[64,1024]{1,0:T(8,128)(2,1)S(1)}, bf16[64,1024]{1,0:T(8,128)(2,1)S(1)}, u32[]{:S(2)}, u32[]{:S(2)}) %collective-permute-start.25) | collective-permute-done | bytes 131104 | tf_op jit(solution)/shard_map/ppermute | solution.py:590
  (85 shorter events, 20.5 us)
Async XLA Ops:
  13.8 7.6 %collective-permute-start.2 = (bf16[2,64,256]{2,1,0:T(8,128)(2,1)S(1)}, bf16[2,64,256]{2,1,0:T(8,128)(2,1)S(1)}, u32[]{:S(2)}, u32[]{:S(2)}) collective-permute-start(bf16[2,64,256]{2,1,0:T(8,128)(2,1)S(1)} %copy-done.4), channel_id=1, source_target_pairs={{16,0},{20,4},{24,8},{17,1},{21,5},{25,9},{18,2},{22,6},{26,10},{1... | collective-permute-start | bytes 196616 | tf_op jit(solution)/shard_map/ppermute | solution.py:507
  15.8 11.7 %collective-permute-start.1 = (bf16[128,1152]{1,0:T(8,128)(2,1)S(1)}, bf16[128,1152]{1,0:T(8,128)(2,1)S(1)}, u32[]{:S(2)}, u32[]{:S(2)}) collective-permute-start(bf16[128,1152]{1,0:T(8,128)(2,1)S(1)} %combine.7.refs_6_.a_ref), channel_id=1, source_target_pairs={{0,8},{4,12},{24,16},{28,20},{1,9},{5,13},{25,17},{29,21},{2,10},{... | collective-permute-start | bytes 884744 | tf_op jit(solution)/shard_map/ppermute | solution.py:492
  34.1 14.3 %collective-permute-start.8 = (bf16[128,1024]{1,0:T(8,128)(2,1)S(1)}, bf16[128,1024]{1,0:T(8,128)(2,1)S(1)}, u32[]{:S(2)}, u32[]{:S(2)}) collective-permute-start(bf16[128,1024]{1,0:T(8,128)(2,1)S(1)} %combine.9.refs_6_), channel_id=1, source_target_pairs={{0,16},{4,20},{1,17},{5,21},{2,18},{6,22},{3,19},{7,23}} | collective-permute-start | bytes 786440 | tf_op jit(solution)/shard_map/ppermute | solution.py:492
  36.0 13.8 %collective-permute-start.3 = (bf16[128,1152]{1,0:T(8,128)(2,1)S(1)}, bf16[128,1152]{1,0:T(8,128)(2,1)S(1)}, u32[]{:S(2)}, u32[]{:S(2)}) collective-permute-start(bf16[128,1152]{1,0:T(8,128)(2,1)S(1)} %combine.8.rest_0_.a_ref), channel_id=1, source_target_pairs={{8,16},{12,20},{16,8},{20,12},{9,17},{13,21},{17,9},{21,13},{10,18... | collective-permute-start | bytes 884744 | tf_op jit(solution)/shard_map/ppermute | solution.py:492
  37.3 14.3 %collective-permute-start.15 = (bf16[128,1152]{1,0:T(8,128)(2,1)S(1)}, bf16[128,1152]{1,0:T(8,128)(2,1)S(1)}, u32[]{:S(2)}, u32[]{:S(2)}) collective-permute-start(bf16[128,1152]{1,0:T(8,128)(2,1)S(1)} %combine.10.refs_6_.a_ref), channel_id=1, source_target_pairs={{0,8},{4,12},{8,0},{12,4},{1,9},{5,13},{9,1},{13,5},{2,10},{6,14},... | collective-permute-start | bytes 884744 | tf_op jit(solution)/shard_map/ppermute | solution.py:492
  48.4 8.3 %collective-permute-start.10 = (bf16[128,1024]{1,0:T(8,128)(2,1)S(1)}, bf16[128,1024]{1,0:T(8,128)(2,1)S(1)}, u32[]{:S(2)}, u32[]{:S(2)}) collective-permute-start(bf16[128,1024]{1,0:T(8,128)(2,1)S(1)} %collective-permute-done.8), channel_id=1, source_target_pairs={{16,24},{20,28},{17,25},{21,29},{18,26},{22,30},{19,27},{23,31}} | collective-permute-start | bytes 786440 | tf_op jit(solution)/shard_map/ppermute | solution.py:492
  49.1 7.6 %collective-permute-start.9 = (bf16[128,1024]{1,0:T(8,128)(2,1)S(1)}, bf16[128,1024]{1,0:T(8,128)(2,1)S(1)}, u32[]{:S(2)}, u32[]{:S(2)}) collective-permute-start(bf16[128,1024]{1,0:T(8,128)(2,1)S(1)} %collective-permute-done.8), channel_id=1, source_target_pairs={{16,8},{20,12},{17,9},{21,13},{18,10},{22,14},{19,11},{23,15}} | collective-permute-start | bytes 786440 | tf_op jit(solution)/shard_map/ppermute | solution.py:492
  50.3 10.1 %collective-permute-start.6 = (bf16[128,1024]{1,0:T(8,128)(2,1)S(1)}, bf16[128,1024]{1,0:T(8,128)(2,1)S(1)}, u32[]{:S(2)}, u32[]{:S(2)}) collective-permute-start(bf16[128,1024]{1,0:T(8,128)(2,1)S(1)} %combine.11.rest_0_), channel_id=1, source_target_pairs={{8,0},{12,4},{16,24},{20,28},{9,1},{13,5},{17,25},{21,29},{10,2},{... | collective-permute-start | bytes 786440 | tf_op jit(solution)/shard_map/ppermute | solution.py:492
  52.6 10.0 %collective-permute-start.20 = (bf16[128,1024]{1,0:T(8,128)(2,1)S(1)}, bf16[128,1024]{1,0:T(8,128)(2,1)S(1)}, u32[]{:S(2)}, u32[]{:S(2)}) collective-permute-start(bf16[128,1024]{1,0:T(8,128)(2,1)S(1)} %combine.13.refs_0_), channel_id=1, source_target_pairs={{0,16},{4,20},{1,17},{5,21},{2,18},{6,22},{3,19},{7,23}} | collective-permute-start | bytes 786440 | tf_op jit(solution)/shard_map/ppermute | solution.py:492
  56.8 8.6 %collective-permute-start.11 = (bf16[128,1024]{1,0:T(8,128)(2,1)S(1)}, bf16[128,1024]{1,0:T(8,128)(2,1)S(1)}, u32[]{:S(2)}, u32[]{:S(2)}) collective-permute-start(bf16[128,1024]{1,0:T(8,128)(2,1)S(1)} %add_select_fusion.refs_2_), channel_id=1, source_target_pairs={{0,4},{4,0},{8,12},{12,8},{16,20},{20,16},{24,28},{28,24},{1,5},{5... | collective-permute-start | bytes 786440 | tf_op jit(solution)/shard_map/ppermute | solution.py:489
  56.9 7.0 %collective-permute-start.16 = (bf16[128,1024]{1,0:T(8,128)(2,1)S(1)}, bf16[128,1024]{1,0:T(8,128)(2,1)S(1)}, u32[]{:S(2)}, u32[]{:S(2)}) collective-permute-start(bf16[128,1024]{1,0:T(8,128)(2,1)S(1)} %combine.12.refs_0_.rest_0_), channel_id=1, source_target_pairs={{8,16},{12,20},{9,17},{13,21},{10,18},{14,22},{11,19},{15,23}} | collective-permute-start | bytes 786440 | tf_op jit(solution)/shard_map/ppermute | solution.py:492
  62.5 10.1 %collective-permute-start.21 = (bf16[128,1024]{1,0:T(8,128)(2,1)S(1)}, bf16[128,1024]{1,0:T(8,128)(2,1)S(1)}, u32[]{:S(2)}, u32[]{:S(2)}) collective-permute-start(bf16[128,1024]{1,0:T(8,128)(2,1)S(1)} %collective-permute-done.20.refs_1_), channel_id=1, source_target_pairs={{16,8},{20,12},{17,9},{21,13},{18,10},{22,14},{19,11},{23,15}} | collective-permute-start | bytes 786440 | tf_op jit(solution)/shard_map/ppermute | solution.py:492
  63.2 9.5 %collective-permute-start.22 = (bf16[128,1024]{1,0:T(8,128)(2,1)S(1)}, bf16[128,1024]{1,0:T(8,128)(2,1)S(1)}, u32[]{:S(2)}, u32[]{:S(2)}) collective-permute-start(bf16[128,1024]{1,0:T(8,128)(2,1)S(1)} %collective-permute-done.20.refs_1_), channel_id=1, source_target_pairs={{16,24},{20,28},{17,25},{21,29},{18,26},{22,30},{19,27},{23,31}} | collective-permute-start | bytes 786440 | tf_op jit(solution)/shard_map/ppermute | solution.py:492
  63.9 14.6 %collective-permute-start.17 = (bf16[128,1024]{1,0:T(8,128)(2,1)S(1)}, bf16[128,1024]{1,0:T(8,128)(2,1)S(1)}, u32[]{:S(2)}, u32[]{:S(2)}) collective-permute-start(bf16[128,1024]{1,0:T(8,128)(2,1)S(1)} %collective-permute-done.16.refs_1_), channel_id=1, source_target_pairs={{16,24},{20,28},{17,25},{21,29},{18,26},{22,30},{19,27},{23,31}} | collective-permute-start | bytes 786440 | tf_op jit(solution)/shard_map/ppermute | solution.py:492
  65.3 5.8 %collective-permute-start.27 = (bf16[1,2,8,256]{3,2,1,0:T(8,128)(2,1)S(1)}, bf16[1,2,8,256]{3,2,1,0:T(8,128)(2,1)S(1)}, u32[]{:S(2)}, u32[]{:S(2)}) collective-permute-start(bf16[1,2,8,256]{3,2,1,0:T(8,128)(2,1)S(1)} %choose.1), channel_id=1, source_target_pairs={{0,4},{4,0},{8,12},{12,8},{16,20},{20,16},{24,28},{28,24},{1,5},{5... | collective-permute-start | bytes 24584 | tf_op jit(solution)/shard_map/ppermute | solution.py:613
  68.9 11.3 %collective-permute-start.12 = (bf16[64,1024]{1,0:T(8,128)(2,1)S(1)}, bf16[64,1024]{1,0:T(8,128)(2,1)S(1)}, u32[]{:S(2)}, u32[]{:S(2)}) collective-permute-start(bf16[64,1024]{1,0:T(8,128)(2,1)S(1)} %get-tuple-element.33), channel_id=1, source_target_pairs={{0,1},{1,0},{2,3},{3,2},{4,5},{5,4},{6,7},{7,6},{8,9},{9,8},{10,11... | collective-permute-start | bytes 393224 | tf_op jit(solution)/shard_map/ppermute | solution.py:590
  71.2 13.7 %collective-permute-start.13 = (bf16[64,1024]{1,0:T(8,128)(2,1)S(1)}, bf16[64,1024]{1,0:T(8,128)(2,1)S(1)}, u32[]{:S(2)}, u32[]{:S(2)}) collective-permute-start(bf16[64,1024]{1,0:T(8,128)(2,1)S(1)} %get-tuple-element.34), channel_id=1, source_target_pairs={{0,2},{1,3},{2,0},{3,1},{4,6},{5,7},{6,4},{7,5},{8,10},{9,11},{10,... | collective-permute-start | bytes 393224 | tf_op jit(solution)/shard_map/ppermute | solution.py:590
  72.7 12.2 %collective-permute-start.14 = (bf16[64,1024]{1,0:T(8,128)(2,1)S(1)}, bf16[64,1024]{1,0:T(8,128)(2,1)S(1)}, u32[]{:S(2)}, u32[]{:S(2)}) collective-permute-start(bf16[64,1024]{1,0:T(8,128)(2,1)S(1)} %get-tuple-element.35), channel_id=1, source_target_pairs={{0,3},{1,2},{2,1},{3,0},{4,7},{5,6},{6,5},{7,4},{8,11},{9,10},{10,... | collective-permute-start | bytes 393224 | tf_op jit(solution)/shard_map/ppermute | solution.py:590
  72.7 7.5 %collective-permute-start.28 = (bf16[2,2,8,256]{3,2,1,0:T(8,128)(2,1)S(1)}, bf16[2,2,8,256]{3,2,1,0:T(8,128)(2,1)S(1)}, u32[]{:S(2)}, u32[]{:S(2)}) collective-permute-start(bf16[2,2,8,256]{3,2,1,0:T(8,128)(2,1)S(1)} %pad_maximum_fusion.3), channel_id=1, source_target_pairs={{0,8},{4,12},{8,0},{12,4},{16,24},{20,28},{24,16},{28,20},{1,9},{5... | collective-permute-start | bytes 49160 | tf_op jit(solution)/shard_map/ppermute | solution.py:613
  78.5 6.4 %collective-permute-start.23 = (bf16[128,1024]{1,0:T(8,128)(2,1)S(1)}, bf16[128,1024]{1,0:T(8,128)(2,1)S(1)}, u32[]{:S(2)}, u32[]{:S(2)}) collective-permute-start(bf16[128,1024]{1,0:T(8,128)(2,1)S(1)} %pick.3.refs_2_), channel_id=1, source_target_pairs={{0,4},{4,0},{8,12},{12,8},{16,20},{20,16},{24,28},{28,24},{1,5},{5... | collective-permute-start | bytes 786440 | tf_op jit(solution)/shard_map/ppermute | solution.py:489
  80.2 9.7 %collective-permute-start.29 = (bf16[4,2,8,256]{3,2,1,0:T(8,128)(2,1)S(1)}, bf16[4,2,8,256]{3,2,1,0:T(8,128)(2,1)S(1)}, u32[]{:S(2)}, u32[]{:S(2)}) collective-permute-start(bf16[4,2,8,256]{3,2,1,0:T(8,128)(2,1)S(1)} %pad_maximum_fusion.2), channel_id=1, source_target_pairs={{0,16},{4,20},{8,24},{12,28},{16,0},{20,4},{24,8},{28,12},{1,17},{... | collective-permute-start | bytes 98312 | tf_op jit(solution)/shard_map/ppermute | solution.py:613
  86.3 5.9 %collective-permute-start.24 = (bf16[64,1024]{1,0:T(8,128)(2,1)S(1)}, bf16[64,1024]{1,0:T(8,128)(2,1)S(1)}, u32[]{:S(2)}, u32[]{:S(2)}) collective-permute-start(bf16[64,1024]{1,0:T(8,128)(2,1)S(1)} %get-tuple-element.38), channel_id=1, source_target_pairs={{0,1},{1,0},{2,3},{3,2},{4,5},{5,4},{6,7},{7,6},{8,9},{9,8},{10,11... | collective-permute-start | bytes 393224 | tf_op jit(solution)/shard_map/ppermute | solution.py:590
  88.3 8.2 %collective-permute-start.25 = (bf16[64,1024]{1,0:T(8,128)(2,1)S(1)}, bf16[64,1024]{1,0:T(8,128)(2,1)S(1)}, u32[]{:S(2)}, u32[]{:S(2)}) collective-permute-start(bf16[64,1024]{1,0:T(8,128)(2,1)S(1)} %get-tuple-element.39), channel_id=1, source_target_pairs={{0,2},{1,3},{2,0},{3,1},{4,6},{5,7},{6,4},{7,5},{8,10},{9,11},{10,... | collective-permute-start | bytes 393224 | tf_op jit(solution)/shard_map/ppermute | solution.py:590
  89.8 6.6 %collective-permute-start.26 = (bf16[64,1024]{1,0:T(8,128)(2,1)S(1)}, bf16[64,1024]{1,0:T(8,128)(2,1)S(1)}, u32[]{:S(2)}, u32[]{:S(2)}) collective-permute-start(bf16[64,1024]{1,0:T(8,128)(2,1)S(1)} %get-tuple-element.40), channel_id=1, source_target_pairs={{0,3},{1,2},{2,1},{3,0},{4,7},{5,6},{6,5},{7,4},{8,11},{9,10},{10,... | collective-permute-start | bytes 393224 | tf_op jit(solution)/shard_map/ppermute | solution.py:590
  (17 other events, 166.9 us)

commit v3 on v2

--- a/solution.py
+++ b/solution.py
@@ -542,14 +542,15 @@
             arrived = send(value[tenant], steps[tenant].pop(0))
             value[tenant] = combine(value[tenant], arrived, not steps[tenant], after)
 
-    def spread(tenant, after=()):
+    def spread(tenant):
         first = max(count[tenant] // 2 - 1, 0)
         last = count[tenant] // 2
-        inside = (chip >= first) & (chip <= last)
         top = (first, last)
         newest = value[tenant]
         if chips == 4 and last == 0:
-            newest = send(newest, [(0, 2)])
+            newest = early.get(tenant, None)
+            if newest is None:
+                newest = send(value[tenant], [(0, 2)])
             held = [newest, send(newest, [(2, 1)]), send(newest, [(2, 3)])]
         else:
             held = []
@@ -563,18 +564,33 @@
                     last += 1
                 newest = send(newest, pairs)
                 held.append(newest)
-        if held and after:
+        return held, top
+
+    def settle(tenant, held, top, after):
+        if held:
             value[tenant] = pick(value[tenant], held, top[0], top[1], after)
-        elif held:
-            value[tenant] = jnp.where(inside, value[tenant], functools.reduce(jnp.add, held))
-
+        whole[tenant] = (value[tenant], swap(value[tenant]))
+
+    chosen = choose(path, draft_kv)
+
+    def gather(after):
+        nonlocal chosen
+        if chosen.shape[0] < n_seq:
+            pairs = [(s, s ^ chosen.shape[0]) for s in range(n_seq)]
+            chosen = stack(chosen, lax.ppermute(chosen, "seq", pairs), after)
+
+    early = {}
     join(3, partial_of(3))
     zero = partial_of(0, [value[3]])
     advance(3, [zero[0]])
     join(0, zero, [value[3]])
-    two = partial_of(2, [value[0]])
+    gather([value[0]])
+    two = partial_of(2, [value[0], chosen])
     join(2, two)
-    one = partial_of(1, [value[2]])
+    gather([value[2]])
+    if chips == 4:
+        early[0] = send(value[0], [(0, 2)])
+    one = partial_of(1, [value[2], chosen] + list(early.values()))
     advance(3, [one[0]])
     advance(2, [value[3]])
     join(1, one, [value[2]])
@@ -592,13 +608,13 @@
         ]
         return own, functools.reduce(jnp.add, arrived, own).astype(BF)
 
-    for tenant in (3, 0):
-        spread(tenant)
-        whole[tenant] = (value[tenant], swap(value[tenant]))
+    moves = {tenant: spread(tenant) for tenant in (2, 1, 0, 3)}
+    first_hop = moves[2][0][:1]
+    settle(0, *moves[0], first_hop)
+    settle(3, *moves[3], [value[0]])
     own, one_sum = sums((3, 0), [])
-    for tenant in (2, 1):
-        spread(tenant, [own])
-        whole[tenant] = (value[tenant], swap(value[tenant]))
+    settle(1, *moves[1], [own])
+    settle(2, *moves[2], [own])
     _, other_sum = sums((2, 1), [one_sum])
 
     assert requests == 2 * n_tp
@@ -607,12 +623,8 @@
         [jnp.where(even, one_sum, other_sum), jnp.where(even, other_sum, one_sum)], axis=0
     )
 
-    chosen = choose(path, draft_kv)
-    distance = 1
-    while distance < n_seq:
-        arrived = lax.ppermute(chosen, "seq", [(s, s ^ distance) for s in range(n_seq)])
-        chosen = jnp.concatenate([chosen, arrived], axis=0)
-        distance *= 2
+    while chosen.shape[0] < n_seq:
+        gather([value[1]])
     new_cache = patched(copy, chosen, lengths, accepted)
     return attn_out, new_cache
 

time: 97.9 us -> 96.3 us (0.984)
  local copies, waits for them, and re-layouts: 9.36 us -> 7.16 us
  waiting for transfers between devices: 12.3 us -> 13.4 us
    unnamed x22 -> x18, local copies, waits for them, and re-layouts: 9.36 us -> 7.16 us
    ppermute x6, waiting for transfers between devices: 4.31 us -> 5.55 us  [sums(): lax.ppermute(other, 'tp', [(t, t ^ k + 1) for t in range(n_tp)]).astype(F32)]
    ppermute x12, starting transfers between devices: 21.8 us -> 20.7 us  [send(): return lax.ppermute(array, 'seq', chip_pairs(pairs))]
  transfers between devices with their start and end apart: 30 -> 30, of which waited for: 7 -> 6; matrix products, arithmetic and copies ran while one was open for 0% -> 0% of each run, Pallas kernels for 20% -> 20%
where the time goes in v3:
time: 96.3 us; the launch traced here: 95.6 us
  starting transfers between devices  42.8 us (44%)
  Pallas kernels  30.1 us (31%)
  waiting for transfers between devices  13.4 us (14%)
  local copies, waits for them, and re-layouts  7.16 us (7%)
  between operations  1.15 us (1%)
    ppermute x12, starting transfers between devices, send(): return lax.ppermute(array, 'seq', chip_pairs(pairs))  20.7 us
    pallas_call x4, Pallas kernels, attend(): pl.pallas_call(functools.partial(attend_kernel, tenant, owners, [used.ind...  19.3 us
    ppermute x3, starting transfers between devices, gather(): chosen = stack(chosen, lax.ppermute(chosen, 'seq', pairs), after)  10.4 us
    ppermute x6, starting transfers between devices, sums(): lax.ppermute(other, 'tp', [(t, t ^ k + 1) for t in range(n_tp)]).astype(F32)  7.33 us
    unnamed x18, local copies, waits for them, and re-layouts  7.16 us
    ppermute x6, waiting for transfers between devices, sums(): lax.ppermute(other, 'tp', [(t, t ^ k + 1) for t in range(n_tp)]).astype(F32)  5.55 us
    ppermute x12, waiting for transfers between devices, send(): return lax.ppermute(array, 'seq', chip_pairs(pairs))  5.29 us
    pallas_call x7, Pallas kernels, combine(): pl.pallas_call(functools.partial(combine_kernel, final), out_shape=jax.Sh...  3.85 us
  transfers between devices with their start and end apart: 30, of which 6 were waited for; matrix products, arithmetic and copies ran while one was open for 0% of the time, Pallas kernels for 20%

profile of v3, /device:TPU:0, one launch (start us, length us, event | category | flops | bytes accessed | tf_op | source)
XLA Modules:
  0.0 95.6 jit_solution(7153714489094423658)
XLA Ops:
  2.4 3.4 %copy-done = bf16[2,8,1024,256]{3,2,1,0:T(8,128)(2,1)S(1)} copy-done((bf16[2,8,1024,256]{3,2,1,0:T(8,128)(2,1)S(1)}, bf16[2,8,1024,256]{3,2,1,0:T(8,128)(2,1)}, u32[]{:S(2)}) %copy-start) | copy-done | bytes 8388632
  5.8 1.6 %copy-done.1 = bf16[512,2048]{1,0:T(8,128)(2,1)S(1)} copy-done((bf16[512,2048]{1,0:T(8,128)(2,1)S(1)}, bf16[512,2048]{1,0:T(8,128)(2,1)}, u32[]{:S(2)}) %copy-start.1) | copy-done | bytes 2097176
  8.9 4.4 %attend_3.1 = (bf16[128,1152]{1,0:T(8,128)(2,1)S(1)}, bf16[128,1152]{1,0:T(8,128)(2,1)S(1)}, bf16[2,8,1024,256]{3,2,1,0:T(8,128)(2,1)}) custom-call(s32[8]{0:T(128)S(1)} %copy-done.4, bf16[512,2048]{1,0:T(8,128)(2,1)S(1)} %copy-done.1, bf16[2,8,1024,256]{3,2,1,0:T(8,128)(2,1)S(1)} %copy-done, f32[8,64,64]{2,1,0:T(8,128)S(1)} %reach.1.refs_3_, ...), custom_call_target="tpu_custom_call" | custom-call | flops 1 | bytes 1 | tf_op jit(solution)/shard_map/attend_3/pallas_call | solution.py:232
  15.8 5.0 %collective-permute-start.1 = (bf16[128,1152]{1,0:T(8,128)(2,1)S(1)}, bf16[128,1152]{1,0:T(8,128)(2,1)S(1)}, u32[]{:S(2)}, u32[]{:S(2)}) collective-permute-start(bf16[128,1152]{1,0:T(8,128)(2,1)S(1)} %combine.7.refs_6_.a_ref), channel_id=1, source_target_pairs={{0,8},{4,12},{24,16},{28,20},{1,9},{5,13},{25,17},{29,21},{2,10},{... | collective-permute-start | bytes 884744 | tf_op jit(solution)/shard_map/ppermute | solution.py:492
  21.4 5.9 %attend_0.1 = (bf16[128,1152]{1,0:T(8,128)(2,1)S(1)}, bf16[128,1152]{1,0:T(8,128)(2,1)S(1)}, bf16[2,8,1024,256]{3,2,1,0:T(8,128)(2,1)}) custom-call(s32[8]{0:T(128)S(1)} %copy-done.4, bf16[512,2048]{1,0:T(8,128)(2,1)S(1)} %copy-done.1, bf16[2,8,1024,256]{3,2,1,0:T(8,128)(2,1)S(1)} %copy-done, ...), custom_call_target="tpu_custom_call", output_to_operand_aliasing={{2}: (7, {})} | custom-call | flops 1 | bytes 1 | tf_op jit(solution)/shard_map/attend_0/pallas_call | solution.py:232
  29.9 4.4 %attend_2.1 = (bf16[128,1152]{1,0:T(8,128)(2,1)S(1)}, bf16[128,1152]{1,0:T(8,128)(2,1)S(1)}, bf16[2,8,1024,256]{3,2,1,0:T(8,128)(2,1)}) custom-call(s32[8]{0:T(128)S(1)} %copy-done.5, bf16[512,2048]{1,0:T(8,128)(2,1)S(1)} %copy-done.1, bf16[2,8,1024,256]{3,2,1,0:T(8,128)(2,1)S(1)} %copy-done, ...), custom_call_target="tpu_custom_call", output_to_operand_aliasing={{2}: (8, {})} | custom-call | flops 1 | bytes 1 | tf_op jit(solution)/shard_map/attend_2/pallas_call | solution.py:232
  34.3 1.6 %collective-permute-start.8 = (bf16[128,1024]{1,0:T(8,128)(2,1)S(1)}, bf16[128,1024]{1,0:T(8,128)(2,1)S(1)}, u32[]{:S(2)}, u32[]{:S(2)}) collective-permute-start(bf16[128,1024]{1,0:T(8,128)(2,1)S(1)} %combine.9.rest_0_.refs_6_.refs_0_), channel_id=1, source_target_pairs={{0,16},{4,20},{1,17},{5,21},{2,18},{6,22},{3,19},{7,23}} | collective-permute-start | bytes 786440 | tf_op jit(solution)/shard_map/ppermute | solution.py:492
  36.0 1.7 %collective-permute-start.7 = (bf16[2,2,8,256]{3,2,1,0:T(8,128)(2,1)S(1)}, bf16[2,2,8,256]{3,2,1,0:T(8,128)(2,1)S(1)}, u32[]{:S(2)}, u32[]{:S(2)}) collective-permute-start(bf16[2,2,8,256]{3,2,1,0:T(8,128)(2,1)S(1)} %stack.3.refs_7_.a_ref), channel_id=1, source_target_pairs={{0,8},{4,12},{8,0},{12,4},{16,24},{20,28},{24,16},{28,20},{1,9},{5... | collective-permute-start | bytes 49160 | tf_op jit(solution)/shard_map/ppermute | solution.py:580
  39.1 3.5 %collective-permute-start.12 = (bf16[128,1152]{1,0:T(8,128)(2,1)S(1)}, bf16[128,1152]{1,0:T(8,128)(2,1)S(1)}, u32[]{:S(2)}, u32[]{:S(2)}) collective-permute-start(bf16[128,1152]{1,0:T(8,128)(2,1)S(1)} %combine.10.rest_0_.refs_6_.a_ref), channel_id=1, source_target_pairs={{0,8},{4,12},{8,0},{12,4},{1,9},{5,13},{9,1},{13,5},{2,10},{6,14},... | collective-permute-start | bytes 884744 | tf_op jit(solution)/shard_map/ppermute | solution.py:492
  42.6 4.6 %attend_1.1 = (bf16[128,1152]{1,0:T(8,128)(2,1)S(1)}, bf16[128,1152]{1,0:T(8,128)(2,1)S(1)}, bf16[2,8,1024,256]{3,2,1,0:T(8,128)(2,1)}) custom-call(s32[8]{0:T(128)S(1)} %copy-done.5, bf16[512,2048]{1,0:T(8,128)(2,1)S(1)} %copy-done.1, bf16[2,8,1024,256]{3,2,1,0:T(8,128)(2,1)S(1)} %copy-done, ...), custom_call_target="tpu_custom_call", output_to_operand_aliasing={{2}: (9, {})} | custom-call | flops 1 | bytes 1 | tf_op jit(solution)/shard_map/attend_1/pallas_call | solution.py:232
  51.5 1.3 %collective-permute-start.9 = (bf16[128,1024]{1,0:T(8,128)(2,1)S(1)}, bf16[128,1024]{1,0:T(8,128)(2,1)S(1)}, u32[]{:S(2)}, u32[]{:S(2)}) collective-permute-start(bf16[128,1024]{1,0:T(8,128)(2,1)S(1)} %combine.11.rest_0_.refs_0_), channel_id=1, source_target_pairs={{8,0},{12,4},{16,24},{20,28},{9,1},{13,5},{17,25},{21,29},{10,2},{... | collective-permute-start | bytes 786440 | tf_op jit(solution)/shard_map/ppermute | solution.py:492
  53.3 4.6 %collective-permute-start.22 = (bf16[128,1024]{1,0:T(8,128)(2,1)S(1)}, bf16[128,1024]{1,0:T(8,128)(2,1)S(1)}, u32[]{:S(2)}, u32[]{:S(2)}) collective-permute-start(bf16[128,1024]{1,0:T(8,128)(2,1)S(1)} %combine.13.refs_0_), channel_id=1, source_target_pairs={{0,16},{4,20},{1,17},{5,21},{2,18},{6,22},{3,19},{7,23}} | collective-permute-start | bytes 786440 | tf_op jit(solution)/shard_map/ppermute | solution.py:492
  58.0 5.0 %collective-permute-done.9.refs_1_ = bf16[128,1024]{1,0:T(8,128)(2,1)S(1)} collective-permute-done((bf16[128,1024]{1,0:T(8,128)(2,1)S(1)}, bf16[128,1024]{1,0:T(8,128)(2,1)S(1)}, u32[]{:S(2)}, u32[]{:S(2)}) %collective-permute-start.9) | collective-permute-done | bytes 262176 | tf_op jit(solution)/shard_map/ppermute | solution.py:492
  65.9 1.4 %project.2 = (f32[64,1024]{1,0:T(8,128)S(1)}, bf16[64,1024]{1,0:T(8,128)(2,1)S(1)}, bf16[64,1024]{1,0:T(8,128)(2,1)S(1)}, bf16[64,1024]{1,0:T(8,128)(2,1)S(1)}) custom-call(bf16[128,1024]{1,0:T(8,128)(2,1)S(1)} %pick.5.refs_0_, bf16[128,1024]{1,0:T(8,128)(2,1)S(1)} %collective-permute-done.14.refs_1_, bf16[128,1024]{1,0:T(8,128)(2,1)S(1)} %pick.4.refs_2_, ...), custom_call_target="tpu_custom_call" | custom-call | flops 1 | bytes 1 | tf_op jit(solution)/shard_map/project/pallas_call | solution.py:332
  67.3 2.2 %collective-permute-start.16 = (bf16[64,1024]{1,0:T(8,128)(2,1)S(1)}, bf16[64,1024]{1,0:T(8,128)(2,1)S(1)}, u32[]{:S(2)}, u32[]{:S(2)}) collective-permute-start(bf16[64,1024]{1,0:T(8,128)(2,1)S(1)} %get-tuple-element.33), channel_id=1, source_target_pairs={{0,1},{1,0},{2,3},{3,2},{4,5},{5,4},{6,7},{7,6},{8,9},{9,8},{10,11... | collective-permute-start | bytes 393224 | tf_op jit(solution)/shard_map/ppermute | solution.py:606
  69.6 1.5 %collective-permute-start.17 = (bf16[64,1024]{1,0:T(8,128)(2,1)S(1)}, bf16[64,1024]{1,0:T(8,128)(2,1)S(1)}, u32[]{:S(2)}, u32[]{:S(2)}) collective-permute-start(bf16[64,1024]{1,0:T(8,128)(2,1)S(1)} %get-tuple-element.34), channel_id=1, source_target_pairs={{0,2},{1,3},{2,0},{3,1},{4,6},{5,7},{6,4},{7,5},{8,10},{9,11},{10,... | collective-permute-start | bytes 393224 | tf_op jit(solution)/shard_map/ppermute | solution.py:606
  71.8 1.7 %collective-permute-done.16 = bf16[64,1024]{1,0:T(8,128)(2,1)S(1)} collective-permute-done((bf16[64,1024]{1,0:T(8,128)(2,1)S(1)}, bf16[64,1024]{1,0:T(8,128)(2,1)S(1)}, u32[]{:S(2)}, u32[]{:S(2)}) %collective-permute-start.16) | collective-permute-done | bytes 131104 | tf_op jit(solution)/shard_map/ppermute | solution.py:606
  73.5 3.9 %collective-permute-done.17 = bf16[64,1024]{1,0:T(8,128)(2,1)S(1)} collective-permute-done((bf16[64,1024]{1,0:T(8,128)(2,1)S(1)}, bf16[64,1024]{1,0:T(8,128)(2,1)S(1)}, u32[]{:S(2)}, u32[]{:S(2)}) %collective-permute-start.17) | collective-permute-done | bytes 131104 | tf_op jit(solution)/shard_map/ppermute | solution.py:606
  77.5 1.4 %project.3 = (f32[64,1024]{1,0:T(8,128)S(1)}, bf16[64,1024]{1,0:T(8,128)(2,1)S(1)}, bf16[64,1024]{1,0:T(8,128)(2,1)S(1)}, bf16[64,1024]{1,0:T(8,128)(2,1)S(1)}) custom-call(bf16[128,1024]{1,0:T(8,128)(2,1)S(1)} %pick.6.refs_0_, bf16[128,1024]{1,0:T(8,128)(2,1)S(1)} %collective-permute-done.20.refs_1_, bf16[128,1024]{1,0:T(8,128)(2,1)S(1)} %pick.7.refs_2_.rest_0_, ...), custom_call_target="tpu_custom_call" | custom-call | flops 1 | bytes 1 | tf_op jit(solution)/shard_map/project/pallas_call | solution.py:332
  78.9 1.3 %collective-permute-start.26 = (bf16[64,1024]{1,0:T(8,128)(2,1)S(1)}, bf16[64,1024]{1,0:T(8,128)(2,1)S(1)}, u32[]{:S(2)}, u32[]{:S(2)}) collective-permute-start(bf16[64,1024]{1,0:T(8,128)(2,1)S(1)} %get-tuple-element.38), channel_id=1, source_target_pairs={{0,1},{1,0},{2,3},{3,2},{4,5},{5,4},{6,7},{7,6},{8,9},{9,8},{10,11... | collective-permute-start | bytes 393224 | tf_op jit(solution)/shard_map/ppermute | solution.py:606
  81.0 1.4 %collective-permute-start.28 = (bf16[64,1024]{1,0:T(8,128)(2,1)S(1)}, bf16[64,1024]{1,0:T(8,128)(2,1)S(1)}, u32[]{:S(2)}, u32[]{:S(2)}) collective-permute-start(bf16[64,1024]{1,0:T(8,128)(2,1)S(1)} %get-tuple-element.40), channel_id=1, source_target_pairs={{0,3},{1,2},{2,1},{3,0},{4,7},{5,6},{6,5},{7,4},{8,11},{9,10},{10,... | collective-permute-start | bytes 393224 | tf_op jit(solution)/shard_map/ppermute | solution.py:606
  82.4 8.2 %collective-permute-start.29 = (bf16[4,2,8,256]{3,2,1,0:T(8,128)(2,1)S(1)}, bf16[4,2,8,256]{3,2,1,0:T(8,128)(2,1)S(1)}, u32[]{:S(2)}, u32[]{:S(2)}) collective-permute-start(bf16[4,2,8,256]{3,2,1,0:T(8,128)(2,1)S(1)} %stack.4.refs_7_.a_ref), channel_id=1, source_target_pairs={{0,16},{4,20},{8,24},{12,28},{16,0},{20,4},{24,8},{28,12},{1,17},{... | collective-permute-start | bytes 98312 | tf_op jit(solution)/shard_map/ppermute | solution.py:580
  90.6 1.9 %collective-permute-done.29.b_ref = bf16[4,2,8,256]{3,2,1,0:T(8,128)(2,1)S(1)} collective-permute-done((bf16[4,2,8,256]{3,2,1,0:T(8,128)(2,1)S(1)}, bf16[4,2,8,256]{3,2,1,0:T(8,128)(2,1)S(1)}, u32[]{:S(2)}, u32[]{:S(2)}) %collective-permute-start.29) | collective-permute-done | bytes 32800 | tf_op jit(solution)/shard_map/ppermute | solution.py:580
  92.5 2.2 %patch_cache.1 = bf16[2,8,1024,256]{3,2,1,0:T(8,128)(2,1)} custom-call(s32[8]{0:T(128)S(1)} %copy-done.5, s32[8]{0:T(128)S(1)} %copy-done.8, bf16[2,8,1024,256]{3,2,1,0:T(8,128)(2,1)} %get-tuple-element.41.cache_ref, bf16[8,2,8,256]{3,2,1,0:T(8,128)(2,1)S(1)} %stack.5.chosen_ref), custom_call_target="tpu_custom_call", output_to_operand_aliasing={{}: (2, {})} | custom-call | tf_op jit(solution)/shard_map/patch_cache/pallas_call | solution.py:461
  (81 shorter events, 20.3 us)
Async XLA Ops:
  13.8 7.6 %collective-permute-start.2 = (bf16[2,64,256]{2,1,0:T(8,128)(2,1)S(1)}, bf16[2,64,256]{2,1,0:T(8,128)(2,1)S(1)}, u32[]{:S(2)}, u32[]{:S(2)}) collective-permute-start(bf16[2,64,256]{2,1,0:T(8,128)(2,1)S(1)} %copy-done.3), channel_id=1, source_target_pairs={{16,0},{20,4},{24,8},{17,1},{21,5},{25,9},{18,2},{22,6},{26,10},{1... | collective-permute-start | bytes 196616 | tf_op jit(solution)/shard_map/ppermute | solution.py:507
  15.8 12.9 %collective-permute-start.1 = (bf16[128,1152]{1,0:T(8,128)(2,1)S(1)}, bf16[128,1152]{1,0:T(8,128)(2,1)S(1)}, u32[]{:S(2)}, u32[]{:S(2)}) collective-permute-start(bf16[128,1152]{1,0:T(8,128)(2,1)S(1)} %combine.7.refs_6_.a_ref), channel_id=1, source_target_pairs={{0,8},{4,12},{24,16},{28,20},{1,9},{5,13},{25,17},{29,21},{2,10},{... | collective-permute-start | bytes 884744 | tf_op jit(solution)/shard_map/ppermute | solution.py:492
  34.3 8.3 %collective-permute-start.8 = (bf16[128,1024]{1,0:T(8,128)(2,1)S(1)}, bf16[128,1024]{1,0:T(8,128)(2,1)S(1)}, u32[]{:S(2)}, u32[]{:S(2)}) collective-permute-start(bf16[128,1024]{1,0:T(8,128)(2,1)S(1)} %combine.9.rest_0_.refs_6_.refs_0_), channel_id=1, source_target_pairs={{0,16},{4,20},{1,17},{5,21},{2,18},{6,22},{3,19},{7,23}} | collective-permute-start | bytes 786440 | tf_op jit(solution)/shard_map/ppermute | solution.py:492
  36.0 6.6 %collective-permute-start.7 = (bf16[2,2,8,256]{3,2,1,0:T(8,128)(2,1)S(1)}, bf16[2,2,8,256]{3,2,1,0:T(8,128)(2,1)S(1)}, u32[]{:S(2)}, u32[]{:S(2)}) collective-permute-start(bf16[2,2,8,256]{3,2,1,0:T(8,128)(2,1)S(1)} %stack.3.refs_7_.a_ref), channel_id=1, source_target_pairs={{0,8},{4,12},{8,0},{12,4},{16,24},{20,28},{24,16},{28,20},{1,9},{5... | collective-permute-start | bytes 49160 | tf_op jit(solution)/shard_map/ppermute | solution.py:580
  37.7 12.2 %collective-permute-start.3 = (bf16[128,1152]{1,0:T(8,128)(2,1)S(1)}, bf16[128,1152]{1,0:T(8,128)(2,1)S(1)}, u32[]{:S(2)}, u32[]{:S(2)}) collective-permute-start(bf16[128,1152]{1,0:T(8,128)(2,1)S(1)} %combine.8.rest_0_.a_ref), channel_id=1, source_target_pairs={{8,16},{12,20},{16,8},{20,12},{9,17},{13,21},{17,9},{21,13},{10,18... | collective-permute-start | bytes 884744 | tf_op jit(solution)/shard_map/ppermute | solution.py:492
  39.1 11.3 %collective-permute-start.12 = (bf16[128,1152]{1,0:T(8,128)(2,1)S(1)}, bf16[128,1152]{1,0:T(8,128)(2,1)S(1)}, u32[]{:S(2)}, u32[]{:S(2)}) collective-permute-start(bf16[128,1152]{1,0:T(8,128)(2,1)S(1)} %combine.10.rest_0_.refs_6_.a_ref), channel_id=1, source_target_pairs={{0,8},{4,12},{8,0},{12,4},{1,9},{5,13},{9,1},{13,5},{2,10},{6,14},... | collective-permute-start | bytes 884744 | tf_op jit(solution)/shard_map/ppermute | solution.py:492
  47.2 5.6 %collective-permute-start.21 = (bf16[128,1152]{1,0:T(8,128)(2,1)S(1)}, bf16[128,1152]{1,0:T(8,128)(2,1)S(1)}, u32[]{:S(2)}, u32[]{:S(2)}) collective-permute-start(bf16[128,1152]{1,0:T(8,128)(2,1)S(1)} %get-tuple-element.36), channel_id=1, source_target_pairs={{0,4},{4,0},{8,12},{12,8},{16,20},{20,16},{24,28},{28,24},{1,5},{5... | collective-permute-start | bytes 884744 | tf_op jit(solution)/shard_map/ppermute | solution.py:489
  48.5 9.4 %collective-permute-start.10 = (bf16[128,1024]{1,0:T(8,128)(2,1)S(1)}, bf16[128,1024]{1,0:T(8,128)(2,1)S(1)}, u32[]{:S(2)}, u32[]{:S(2)}) collective-permute-start(bf16[128,1024]{1,0:T(8,128)(2,1)S(1)} %collective-permute-done.8.refs_8_.refs_1_), channel_id=1, source_target_pairs={{16,8},{20,12},{17,9},{21,13},{18,10},{22,14},{19,11},{23,15}} | collective-permute-start | bytes 786440 | tf_op jit(solution)/shard_map/ppermute | solution.py:492
  49.2 8.7 %collective-permute-start.11 = (bf16[128,1024]{1,0:T(8,128)(2,1)S(1)}, bf16[128,1024]{1,0:T(8,128)(2,1)S(1)}, u32[]{:S(2)}, u32[]{:S(2)}) collective-permute-start(bf16[128,1024]{1,0:T(8,128)(2,1)S(1)} %collective-permute-done.8.refs_8_.refs_1_), channel_id=1, source_target_pairs={{16,24},{20,28},{17,25},{21,29},{18,26},{22,30},{19,27},{23,31}} | collective-permute-start | bytes 786440 | tf_op jit(solution)/shard_map/ppermute | solution.py:492
  50.9 7.1 %collective-permute-start.13 = (bf16[128,1024]{1,0:T(8,128)(2,1)S(1)}, bf16[128,1024]{1,0:T(8,128)(2,1)S(1)}, u32[]{:S(2)}, u32[]{:S(2)}) collective-permute-start(bf16[128,1024]{1,0:T(8,128)(2,1)S(1)} %combine.12.refs_0_.rest_0_), channel_id=1, source_target_pairs={{8,16},{12,20},{9,17},{13,21},{10,18},{14,22},{11,19},{15,23}} | collective-permute-start | bytes 786440 | tf_op jit(solution)/shard_map/ppermute | solution.py:492
  51.5 11.5 %collective-permute-start.9 = (bf16[128,1024]{1,0:T(8,128)(2,1)S(1)}, bf16[128,1024]{1,0:T(8,128)(2,1)S(1)}, u32[]{:S(2)}, u32[]{:S(2)}) collective-permute-start(bf16[128,1024]{1,0:T(8,128)(2,1)S(1)} %combine.11.rest_0_.refs_0_), channel_id=1, source_target_pairs={{8,0},{12,4},{16,24},{20,28},{9,1},{13,5},{17,25},{21,29},{10,2},{... | collective-permute-start | bytes 786440 | tf_op jit(solution)/shard_map/ppermute | solution.py:492
  53.3 10.5 %collective-permute-start.22 = (bf16[128,1024]{1,0:T(8,128)(2,1)S(1)}, bf16[128,1024]{1,0:T(8,128)(2,1)S(1)}, u32[]{:S(2)}, u32[]{:S(2)}) collective-permute-start(bf16[128,1024]{1,0:T(8,128)(2,1)S(1)} %combine.13.refs_0_), channel_id=1, source_target_pairs={{0,16},{4,20},{1,17},{5,21},{2,18},{6,22},{3,19},{7,23}} | collective-permute-start | bytes 786440 | tf_op jit(solution)/shard_map/ppermute | solution.py:492
  63.9 7.2 %collective-permute-start.23 = (bf16[128,1024]{1,0:T(8,128)(2,1)S(1)}, bf16[128,1024]{1,0:T(8,128)(2,1)S(1)}, u32[]{:S(2)}, u32[]{:S(2)}) collective-permute-start(bf16[128,1024]{1,0:T(8,128)(2,1)S(1)} %collective-permute-done.22.refs_1_), channel_id=1, source_target_pairs={{16,8},{20,12},{17,9},{21,13},{18,10},{22,14},{19,11},{23,15}} | collective-permute-start | bytes 786440 | tf_op jit(solution)/shard_map/ppermute | solution.py:492
  64.5 6.6 %collective-permute-start.24 = (bf16[128,1024]{1,0:T(8,128)(2,1)S(1)}, bf16[128,1024]{1,0:T(8,128)(2,1)S(1)}, u32[]{:S(2)}, u32[]{:S(2)}) collective-permute-start(bf16[128,1024]{1,0:T(8,128)(2,1)S(1)} %collective-permute-done.22.refs_1_), channel_id=1, source_target_pairs={{16,24},{20,28},{17,25},{21,29},{18,26},{22,30},{19,27},{23,31}} | collective-permute-start | bytes 786440 | tf_op jit(solution)/shard_map/ppermute | solution.py:492
  65.2 6.0 %collective-permute-start.19 = (bf16[128,1024]{1,0:T(8,128)(2,1)S(1)}, bf16[128,1024]{1,0:T(8,128)(2,1)S(1)}, u32[]{:S(2)}, u32[]{:S(2)}) collective-permute-start(bf16[128,1024]{1,0:T(8,128)(2,1)S(1)} %collective-permute-done.13.refs_4_.refs_1_), channel_id=1, source_target_pairs={{16,24},{20,28},{17,25},{21,29},{18,26},{22,30},{19,27},{23,31}} | collective-permute-start | bytes 786440 | tf_op jit(solution)/shard_map/ppermute | solution.py:492
  67.3 6.1 %collective-permute-start.16 = (bf16[64,1024]{1,0:T(8,128)(2,1)S(1)}, bf16[64,1024]{1,0:T(8,128)(2,1)S(1)}, u32[]{:S(2)}, u32[]{:S(2)}) collective-permute-start(bf16[64,1024]{1,0:T(8,128)(2,1)S(1)} %get-tuple-element.33), channel_id=1, source_target_pairs={{0,1},{1,0},{2,3},{3,2},{4,5},{5,4},{6,7},{7,6},{8,9},{9,8},{10,11... | collective-permute-start | bytes 393224 | tf_op jit(solution)/shard_map/ppermute | solution.py:606
  69.6 7.8 %collective-permute-start.17 = (bf16[64,1024]{1,0:T(8,128)(2,1)S(1)}, bf16[64,1024]{1,0:T(8,128)(2,1)S(1)}, u32[]{:S(2)}, u32[]{:S(2)}) collective-permute-start(bf16[64,1024]{1,0:T(8,128)(2,1)S(1)} %get-tuple-element.34), channel_id=1, source_target_pairs={{0,2},{1,3},{2,0},{3,1},{4,6},{5,7},{6,4},{7,5},{8,10},{9,11},{10,... | collective-permute-start | bytes 393224 | tf_op jit(solution)/shard_map/ppermute | solution.py:606
  71.1 6.3 %collective-permute-start.18 = (bf16[64,1024]{1,0:T(8,128)(2,1)S(1)}, bf16[64,1024]{1,0:T(8,128)(2,1)S(1)}, u32[]{:S(2)}, u32[]{:S(2)}) collective-permute-start(bf16[64,1024]{1,0:T(8,128)(2,1)S(1)} %get-tuple-element.35), channel_id=1, source_target_pairs={{0,3},{1,2},{2,1},{3,0},{4,7},{5,6},{6,5},{7,4},{8,11},{9,10},{10,... | collective-permute-start | bytes 393224 | tf_op jit(solution)/shard_map/ppermute | solution.py:606
  71.2 6.3 %collective-permute-start.25 = (bf16[128,1024]{1,0:T(8,128)(2,1)S(1)}, bf16[128,1024]{1,0:T(8,128)(2,1)S(1)}, u32[]{:S(2)}, u32[]{:S(2)}) collective-permute-start(bf16[128,1024]{1,0:T(8,128)(2,1)S(1)} %pick.7.refs_2_.rest_0_), channel_id=1, source_target_pairs={{0,4},{4,0},{8,12},{12,8},{16,20},{20,16},{24,28},{28,24},{1,5},{5... | collective-permute-start | bytes 786440 | tf_op jit(solution)/shard_map/ppermute | solution.py:489
  71.3 6.2 %collective-permute-start.20 = (bf16[128,1024]{1,0:T(8,128)(2,1)S(1)}, bf16[128,1024]{1,0:T(8,128)(2,1)S(1)}, u32[]{:S(2)}, u32[]{:S(2)}) collective-permute-start(bf16[128,1024]{1,0:T(8,128)(2,1)S(1)} %pick.6.refs_0_), channel_id=1, source_target_pairs={{0,4},{4,0},{8,12},{12,8},{16,20},{20,16},{24,28},{28,24},{1,5},{5... | collective-permute-start | bytes 786440 | tf_op jit(solution)/shard_map/ppermute | solution.py:489
  78.9 15.9 %collective-permute-start.26 = (bf16[64,1024]{1,0:T(8,128)(2,1)S(1)}, bf16[64,1024]{1,0:T(8,128)(2,1)S(1)}, u32[]{:S(2)}, u32[]{:S(2)}) collective-permute-start(bf16[64,1024]{1,0:T(8,128)(2,1)S(1)} %get-tuple-element.38), channel_id=1, source_target_pairs={{0,1},{1,0},{2,3},{3,2},{4,5},{5,4},{6,7},{7,6},{8,9},{9,8},{10,11... | collective-permute-start | bytes 393224 | tf_op jit(solution)/shard_map/ppermute | solution.py:606
  80.2 14.6 %collective-permute-start.27 = (bf16[64,1024]{1,0:T(8,128)(2,1)S(1)}, bf16[64,1024]{1,0:T(8,128)(2,1)S(1)}, u32[]{:S(2)}, u32[]{:S(2)}) collective-permute-start(bf16[64,1024]{1,0:T(8,128)(2,1)S(1)} %get-tuple-element.39), channel_id=1, source_target_pairs={{0,2},{1,3},{2,0},{3,1},{4,6},{5,7},{6,4},{7,5},{8,10},{9,11},{10,... | collective-permute-start | bytes 393224 | tf_op jit(solution)/shard_map/ppermute | solution.py:606
  81.0 13.8 %collective-permute-start.28 = (bf16[64,1024]{1,0:T(8,128)(2,1)S(1)}, bf16[64,1024]{1,0:T(8,128)(2,1)S(1)}, u32[]{:S(2)}, u32[]{:S(2)}) collective-permute-start(bf16[64,1024]{1,0:T(8,128)(2,1)S(1)} %get-tuple-element.40), channel_id=1, source_target_pairs={{0,3},{1,2},{2,1},{3,0},{4,7},{5,6},{6,5},{7,4},{8,11},{9,10},{10,... | collective-permute-start | bytes 393224 | tf_op jit(solution)/shard_map/ppermute | solution.py:606
  82.4 10.1 %collective-permute-start.29 = (bf16[4,2,8,256]{3,2,1,0:T(8,128)(2,1)S(1)}, bf16[4,2,8,256]{3,2,1,0:T(8,128)(2,1)S(1)}, u32[]{:S(2)}, u32[]{:S(2)}) collective-permute-start(bf16[4,2,8,256]{3,2,1,0:T(8,128)(2,1)S(1)} %stack.4.refs_7_.a_ref), channel_id=1, source_target_pairs={{0,16},{4,20},{8,24},{12,28},{16,0},{20,4},{24,8},{28,12},{1,17},{... | collective-permute-start | bytes 98312 | tf_op jit(solution)/shard_map/ppermute | solution.py:580
  (15 other events, 99.3 us)
